TPU v7x, 128 devices: a whole 4x4x4 slice. The times are simulated.
128 devices in a mesh: grp: 8 (over z_hi, y), tp: 16 (over z_lo, x, core).
Axes of the slice: x: 4, y: 4, z: 4 (z_hi: 2, z_lo: 2; z = z_hi * 2 + z_lo), core: 2. Of those that a mesh axis runs over, the one named last changes fastest.
Arguments:
- hidden: bfloat16 [12288, 8192], P(('grp', 'tp')), may hold values from -21 to 21
- boundaries: int32 [8, 128], P('grp'), may hold values from 0 to 1535, as said below
- wq_old: bfloat16 [8192, 4096], P(None, 'tp'), may hold values from -0.0625 to 0.0625
- wk_old: bfloat16 [8192, 512], P(None, 'tp'), may hold values from -0.0625 to 0.0625
- wv_old: bfloat16 [8192, 512], P(None, 'tp'), may hold values from -0.0625 to 0.0625
- wo_old: bfloat16 [4096, 8192], P('tp'), may hold values from -0.125 to 0.125
- weights: bfloat16 [8192, 4096], P(('grp', 'tp')), may hold values from -0.0625 to 0.0625
- grads: bfloat16 [8192, 4096], P(('grp', 'tp')), may hold values from -0.15625 to 0.15625
- moment: float32 [8192, 4096], P(('grp', 'tp')), may hold values from -0.015625 to 0.015625
- second: float32 [8192, 4096], P(('grp', 'tp')), may hold values from 1e-08 to 4e-07
Outputs:
- step_features: bfloat16 [1024, 8192], P('grp', 'tp')
- quantized: bfloat16 [8192, 4096], P(None, 'tp')
- scales: float32 [64, 32], P(None, 'tp')
Inputs may be any that keep to these rules, and one draw needn't show every extreme that they name: `boundaries`: each row is strictly increasing and ends at 1535.
All inputs are finite; a program needn't handle non-finite values.
Results may differ from a plain program's by a relative error of at most 0.024.
The roundings to bfloat16 on the way count: a program that leaves them out, or rounds other values in their place, can miss the bound.
Values may be sent and summed in bfloat16 or wider, within the bound.
No kernel may reach another device: no remote copies, remote signals or barrier semaphores. Data moves between devices by JAX's collectives and lax.ppermute only.
A program may use at most 128 MiB of HBM per device.

v0:
```python
import jax
import jax.numpy as jnp
from jax import lax
from jax.experimental import pallas as pl
from jax.experimental.pallas import tpu as pltpu
from jax.sharding import PartitionSpec as P

HD = 128
BLOCK = 128
TOK = 96
WIDE = 8192
STEPS = 128
AXES = ("grp", "tp")
X_GROUPS = [[8 * a + 2 * e + c for e in range(4)] for a in range(2) for c in range(2)]
ZX_GROUPS = [[2 * e + c for e in range(8)] for c in range(2)]
Y_GROUPS = [[4 * a + b for b in range(4)] for a in range(2)]
F32 = jnp.float32
BF16 = jnp.bfloat16


def coords(i):
    return (i // 64, i // 16 % 4, i // 8 % 2, i // 2 % 4, i % 2)


def send(value, zh=0, y=0, zl=0, x=0, core=0):
    pairs = []
    for i in range(128):
        a, b, l, e, c = coords(i)
        j = ((((a ^ zh) * 4 + (b + y) % 4) * 2 + (l ^ zl)) * 4 + (e + x) % 4) * 2 + (c ^ core)
        pairs.append((i, j))
    return lax.ppermute(value, AXES, pairs)


def swap_all(value, axis, groups):
    return lax.all_to_all(value, axis, split_axis=0, concat_axis=0, axis_index_groups=groups, tiled=True)


def after(value, *others):
    return lax.optimization_barrier((value, *others))[0]


def place():
    ti = lax.axis_index("tp")
    return ti // 8, ti // 2 % 4, ti % 2


def column(bound_ref):
    row = lax.broadcasted_iota(jnp.int32, (STEPS, STEPS), 0)
    lane = lax.broadcasted_iota(jnp.int32, (STEPS, STEPS), 1)
    spread = jnp.where(row == lane, bound_ref[...].astype(F32), 0.0)
    return jnp.sum(spread, axis=1, keepdims=True).astype(jnp.int32)


def nt_dot(a, b):
    return lax.dot_general(a, b, (((1,), (1,)), ((), ())), preferred_element_type=F32)


ANY = pl.BlockSpec(memory_space=pl.ANY)
HBM = pl.BlockSpec(memory_space=pltpu.HBM)
VMEM = pl.BlockSpec(memory_space=pltpu.VMEM)


def move(args, outs, cost=100, vmem=24):
    def wrap(body, count):
        def run(*refs):
            for copy in fetch(body(*refs[:-1]), refs[-1]):
                copy.wait()

        return call(
            run, outs, *args, in_specs=[ANY] * len(args), out_specs=[VMEM] * len(outs),
            scratch_shapes=[pltpu.SemaphoreType.DMA((count,))], cost=cost, vmem=vmem,
        )

    return wrap


def fetch(pairs, sems):
    copies = [pltpu.make_async_copy(src, dst, sems.at[i]) for i, (src, dst) in enumerate(pairs)]
    for copy in copies:
        copy.start()
    return copies


def call(body, outs, *args, vmem=24, cost=0, **kw):
    return pl.pallas_call(
        body,
        out_shape=outs,
        cost_estimate=pl.CostEstimate(flops=cost * 10**9, bytes_accessed=0, transcendentals=0),
        compiler_params=pltpu.CompilerParams(vmem_limit_bytes=vmem * 2**20),
        **kw,
    )(*args)


def shape(*dims, dtype=BF16):
    return jax.ShapeDtypeStruct(dims, dtype)


def join_body(top_any, low_any, out_ref, sems):
    for copy in fetch([(top_any, out_ref.at[pl.ds(0, 32)]), (low_any, out_ref.at[pl.ds(32, 32)])], sems):
        copy.wait()


def token_body(_, out_ref):
    out_ref[...] = jnp.zeros((8, BLOCK), F32)


def first_body(w_any, g_any, m_any, s_any, own_any, oth_any, bound_ref, out_ref, w_ref, g_ref, m_ref, s_ref, own_ref, oth_ref, sems):
    zl, xx, cc = place()
    half = pl.ds(pl.multiple_of(cc * 4096, 4096), 4096)
    pairs = [(own_any.at[:, half], own_ref), (oth_any.at[:, half], oth_ref), (w_any, w_ref), (g_any, g_ref)]
    for i in range(2):
        rows = pl.ds(32 * i, 32)
        pairs += [(m_any.at[rows], m_ref.at[rows]), (s_any.at[rows], s_ref.at[rows])]
    copies = fetch(pairs, sems)
    corr_one = 1.0 - 0.9**10
    corr_two = 1.0 - 0.999**10
    base = (zl * 8 + xx * 2) * TOK
    spot = lax.broadcasted_iota(jnp.int32, (STEPS, TOK), 1)
    bound = column(bound_ref)
    one = (bound == base + cc * TOK + spot).astype(BF16)
    two = (bound == base + (1 - cc) * TOK + spot).astype(BF16)
    for copy in copies[:2]:
        copy.wait()
    for x in range(4):
        at = slice(x * 1024, (x + 1) * 1024)
        part = jnp.dot(one, own_ref[:, at], preferred_element_type=F32)
        part += jnp.dot(two, oth_ref[:, at], preferred_element_type=F32)
        out_ref[x, :STEPS] = part.astype(BF16)
    for copy in copies[2:]:
        copy.wait()
    for x in range(4):
        for r in range(2):
            for k in range(2):
                col = (((zl ^ r) * 4 + x) * 2 + (cc ^ k)) * 256
                at = pl.ds(pl.multiple_of(col, 256), 256)
                wfull = w_ref[:, at].astype(F32)
                gfull = g_ref[:, at].astype(F32)
                first_new = 0.9 * m_ref[:, at] + 0.1 * gfull
                second_new = 0.999 * s_ref[:, at] + 0.001 * gfull * gfull
                update = first_new / corr_one / (jnp.sqrt(second_new / corr_two) + 1e-08)
                fresh = (wfull - 0.02 * (update + 0.1 * wfull)).astype(BF16)
                out_ref[x, STEPS:, (r * 2 + k) * 256:(r * 2 + k + 1) * 256] = fresh


def middle_body(got_any, acc_ref, keep_ref, give_ref, got_ref, sems):
    for copy in fetch([(got_any.at[x], got_ref.at[x]) for x in range(4)], sems):
        copy.wait()
    acc = got_ref[0, :STEPS] + got_ref[1, :STEPS] + got_ref[2, :STEPS] + got_ref[3, :STEPS]
    for i in range(4):
        acc_ref[i * STEPS:(i + 1) * STEPS] = acc[:, i * 256:(i + 1) * 256]
    for r in range(2):
        for x in range(4):
            row = (r * 4 + x) * 64
            keep_ref[row:row + 64] = got_ref[x, STEPS:, r * 512:r * 512 + 256]
            give_ref[row:row + 64] = got_ref[x, STEPS:, r * 512 + 256:(r + 1) * 512]


def spread_pairs(keep, taken, near, far):
    pairs = []
    for k, ref in enumerate((keep, taken)):
        pairs.append((ref.at[pl.ds(0, 256)], near.at[pl.ds(k * 256, 256)]))
        pairs.append((ref.at[pl.ds(256, 256)], far.at[pl.ds(k * 256, 256)]))
    return pairs


def chunk_pairs(*refs):
    return [(ref, refs[-1].at[pl.ds(i * 512, 512)]) for i, ref in enumerate(refs[:-1])]


def on_pairs(up, down, first, second):
    return [(up.at[pl.ds(0, 1024)], first), (down.at[pl.ds(1024, 1024)], second)]


def line_pairs(k0, k1, k2, k3, kv_ref):
    return [(ref, kv_ref.at[:, pl.ds(x * 4 * TOK, 4 * TOK)]) for x, ref in enumerate((k0, k1, k2, k3))]


def share_body(mine_any, got_any, out_ref, mine_ref, got_ref, sems):
    for copy in fetch([(mine_any, mine_ref), (got_any, got_ref)], sems):
        copy.wait()
    for i in range(4):
        rows = slice(i * STEPS, (i + 1) * STEPS)
        block = mine_ref[rows] + got_ref[rows]
        for x in range(4):
            out_ref[x, :, i * 256:(i + 1) * 256] = block


def quant_body(at_ref, *refs):
    parts, (q_any, s_ref, q_ref, sems) = refs[:2], refs[-4:]
    zl, cc = at_ref[1], at_ref[2]
    lane = lax.broadcasted_iota(jnp.int32, (1, 64), 1)
    scales = [refs[3][n:n + 1, :] if len(refs) > 6 else jnp.zeros((1, 64), F32) for n in range(2)]
    copies = []
    for z in range(2):
        part = parts[z].at[parts[z].shape[0] // 2 * z]
        spot = (at_ref[0] ^ z) * 4 + at_ref[3]
        for r in range(2):
            for x in range(4):
                block = (zl ^ r) * 4 + x
                row_a = pl.multiple_of(block * BLOCK + cc * 64, 64)
                row_b = pl.multiple_of(block * BLOCK + (1 - cc) * 64, 64)
                mine, other = part[r, 0, x].astype(F32), part[r, 1, x].astype(F32)
                for n in range(2):
                    cols = slice(n * BLOCK, (n + 1) * BLOCK)
                    a, b = mine[:, cols], other[:, cols]
                    amax = jnp.max(jnp.maximum(jnp.abs(a), jnp.abs(b)), axis=(0, 1), keepdims=True) + 1e-06
                    factor = 448.0 / amax
                    q_ref[z, pl.ds(row_a, 64), cols] = (a * factor).astype(BF16)
                    q_ref[z, pl.ds(row_b, 64), cols] = (b * factor).astype(BF16)
                    scales[n] = jnp.where(lane == spot * 8 + block, amax / 448.0, scales[n])
        rows = pl.ds(pl.multiple_of(spot * 1024, 1024), 1024)
        copies += fetch([(q_ref.at[z], q_any.at[rows])], sems.at[pl.ds(z, 1)])
    for n in range(2):
        s_ref[n:n + 1, :] = scales[n]
    for copy in copies:
        copy.wait()


def quantize(parts, at, before):
    return call(
        quant_body, [shape(8192, 256), shape(2, 64, dtype=F32)], at, *parts, *before,
        in_specs=[pl.BlockSpec(memory_space=pltpu.SMEM)] + [VMEM] * 2 + [ANY, VMEM][:len(before)],
        out_specs=[ANY, VMEM],
        input_output_aliases={3: 0} if before else {},
        scratch_shapes=[pltpu.VMEM((2, 1024, 256), BF16), pltpu.SemaphoreType.DMA((2,))],
    )


def kv_body(own, oth, zown, zoth, k0, v0, k1, v1, k2v3, v2, k3, o0, o1, o2, o3, acc, tok, wall, sems):
    _, xx, cc = place()
    copies = []
    for e in range(4):
        at = pl.ds(e * 2048, 2048)
        pairs = [(r.at[:, at], tok.at[e, pl.ds(i * TOK, TOK)]) for i, r in enumerate((own, oth, zown, zoth))]
        k2, v3 = k2v3.at[pl.ds(0, 32)], k2v3.at[pl.ds(32, 32)]
        for i, r in enumerate((k0, v0, k1, v1, k2, v2, k3, v3)):
            pairs.append((r.at[:, at], wall.at[e, pl.ds(i * 32, 32)]))
        copies.append(fetch(pairs, sems.at[e]))
    for e in range(4):
        for copy in copies[e]:
            copy.wait()
        part = nt_dot(wall[e], tok[e])
        if e == 0:
            acc[...] = part
        else:
            acc[...] += part
    total = acc[...]
    swapped = jnp.concatenate([total[:, i * TOK:(i + 1) * TOK] for i in (1, 0, 3, 2)], 1)
    acc[...] = jnp.where(cc == 0, total, swapped)
    for d, out in enumerate((o0, o1, o2, o3)):
        target = (xx + d) % 4
        for b in range(2):
            row = (target // 2 * 2 + b - xx) % 4 * 64
            out[b * 32:(b + 1) * 32] = acc[pl.ds(pl.multiple_of(row, 32), 32), :].astype(BF16)
            out[64 + b * 32:64 + (b + 1) * 32] = acc[pl.ds(pl.multiple_of(row + 32, 32), 32), :].astype(BF16)


def project(ctx_ref, wo_ref, core, i):
    block = wo_ref[:, pl.ds(pl.multiple_of((i * 2 + core) * 512, 512), 512)]
    return jnp.dot(ctx_ref[...], block, preferred_element_type=F32).astype(BF16)


def attend_body(rows_any, rows_oth, wq_any, half_any, other_any, bound_ref, wo_any, _, out_a, out_b, mine_any,
                ctx_ref, half_ref, other_ref, wo_ref, stage, rows_ref, wq_ref, kv_sems, wo_sems, out_sems, row_sems, wq_sems):
    zl, xx, cc = place()
    first = cc == 0
    outs = (out_a, out_b)
    pairs = [((rows_any, rows_oth)[i // 4].at[i % 4], rows_ref.at[i]) for i in range(8)]
    row_copies = fetch(pairs, row_sems)
    pairs = []
    for i in range(16):
        row = (cc * 8 + i) % 16 * 512
        pairs.append((wq_any.at[pl.ds(pl.multiple_of(row, 512), 512)], wq_ref.at[pl.ds(i * 512, 512)]))
    wq_copies = fetch(pairs, wq_sems)
    kv_copies = fetch([(half_any, half_ref), (other_any, other_ref)], kv_sems)
    wo_copies = fetch([(wo_any.at[pl.ds(i * 16, 16)], wo_ref.at[pl.ds(i * 16, 16)]) for i in range(16)], wo_sems)
    queries = jnp.zeros((STEPS, 256), F32)
    for i in range(8):
        row_copies[i].wait()
        wq_copies[2 * i].wait()
        wq_copies[2 * i + 1].wait()
        queries += jnp.dot(rows_ref[i], wq_ref[i * 1024:(i + 1) * 1024, :], preferred_element_type=F32)
    queries = queries.astype(BF16)
    for copy in kv_copies:
        copy.wait()

    def merged(base):
        parts = []
        for b in range(2):
            rows = slice(base + b * 32, base + (b + 1) * 32)
            m, o = half_ref[rows], other_ref[rows]
            parts += [jnp.where(first, m, o), jnp.where(first, o, m)]
        return jnp.concatenate(parts, 0)

    keys, values = merged(0), merged(64)
    slot = lax.broadcasted_iota(jnp.int32, (STEPS, 16 * TOK), 1)
    sx = jnp.where(slot >= 4 * TOK, 1, 0) + jnp.where(slot >= 8 * TOK, 1, 0) + jnp.where(slot >= 12 * TOK, 1, 0)
    rest = slot - sx * (4 * TOK)
    sr = jnp.where(rest >= 2 * TOK, 1, 0)
    position = ((zl ^ sr) * 8 + ((xx + sx) & 3) * 2) * TOK + rest - sr * (2 * TOK)
    visible = position <= column(bound_ref)
    for h in range(2):
        scores = jnp.dot(queries[:, h * HD:(h + 1) * HD], keys, preferred_element_type=F32)
        scores = scores * (1.0 / jnp.sqrt(F32(HD)))
        scores = jnp.where(visible, scores, F32(-1e30))
        expo = jnp.exp(scores - jnp.max(scores, axis=-1, keepdims=True))
        probs = (expo / jnp.sum(expo, axis=-1, keepdims=True)).astype(BF16)
        ctx_ref[:, h * HD:(h + 1) * HD] = nt_dot(probs, values).astype(BF16)
    for copy in wo_copies:
        copy.wait()
    leaving = []
    for i in range(8):
        stage[i] = project(ctx_ref, wo_ref, 1 - cc, i)
        leaving.append(leave((stage.at[i], outs[i // 4].at[i % 4]), out_sems, i))
    for i in range(8):
        stage[8 + i] = project(ctx_ref, wo_ref, cc, i)
        leaving.append(leave((stage.at[8 + i], mine_any.at[i]), out_sems, 8 + i))
    for copy in leaving:
        copy.wait()


def leave(blocks, sems, i):
    copy = pltpu.make_async_copy(*blocks, sems.at[i])
    copy.start()
    return copy


def add_body(mine_any, got_a, got_b, out_any, mine_ref, got_ref, stage, sems, out_sems):
    pairs = []
    for i in range(8):
        pairs += [(mine_any.at[i], mine_ref.at[i]), ((got_a, got_b)[i // 4].at[i % 4], got_ref.at[i])]
    copies = fetch(pairs, sems)
    leaving = []
    for i in range(8):
        copies[2 * i].wait()
        copies[2 * i + 1].wait()
        stage[i] = (mine_ref[i].astype(F32) + got_ref[i].astype(F32)).astype(BF16)
        leaving.append(leave((stage.at[i], out_any.at[i]), out_sems, i))
    for copy in leaving:
        copy.wait()


def final_body(got_ref, out_ref):
    total = got_ref[0].astype(F32)
    for i in range(1, 8):
        total += got_ref[i].astype(F32)
    out_ref[...] = total.astype(BF16)


def on_device(hidden, boundaries, wq_old, wk_old, wv_old, wo_old, weights, grads, moment, second):
    bounds = boundaries
    gi = lax.axis_index("grp")
    zl, xx, cc = place()

    zown = send(hidden, zl=1)
    oth = send(hidden, core=1)
    k0 = wk_old.T
    k3, k1 = send(k0, x=1), send(k0, x=-1)

    (parts,) = call(
        first_body, [shape(4, 192, 1024)], weights, grads, moment, second, hidden, oth, bounds,
        in_specs=[HBM] * 6 + [VMEM],
        scratch_shapes=[pltpu.VMEM((64, 4096), BF16)] * 2 + [pltpu.VMEM((64, 4096), F32)] * 2
        + [pltpu.VMEM((TOK, 4096), BF16)] * 2 + [pltpu.SemaphoreType.DMA((8,))],
        cost=100, vmem=60,
    )
    got = swap_all(parts, "tp", X_GROUPS)
    v0 = wv_old.T
    (joined,) = call(
        join_body, [shape(64, WIDE)], after(k3, k1, parts), v0, in_specs=[HBM] * 2, vmem=60, cost=100,
        scratch_shapes=[pltpu.SemaphoreType.DMA((2,))],
    )
    k2v3 = send(joined, x=1)
    v1 = send(after(v0, joined), x=-1)
    got = after(got, joined)
    acc, keep, give = call(
        middle_body, [shape(512, 256)] * 3, got, cost=100,
        in_specs=[ANY],
        scratch_shapes=[pltpu.VMEM((4, 192, 1024), BF16), pltpu.SemaphoreType.DMA((4,))],
    )
    from_zl = send(acc, zl=1)
    got_core = send(give, core=1)

    zoth = send(zown, core=1)
    (shared,) = call(share_body, [shape(4, STEPS, 1024)], acc, from_zl, in_specs=[ANY] * 2,
        scratch_shapes=[pltpu.VMEM((512, 256), BF16)] * 2 + [pltpu.SemaphoreType.DMA((2,))],
    )
    v2 = send(after(v1, shared), x=-1)
    rows_half = swap_all(shared, "tp", X_GROUPS)
    near, far = move([after(keep, shared), got_core], [shape(512, 256)] * 2, cost=0)(spread_pairs, 4)
    far_zl, near_zh, far_zh = send(far, zl=1), send(near, zh=1), send(far, zh=1, zl=1)

    zboth = after((zown, zoth), shared)
    kv = call(
        kv_body, [shape(128, 4 * TOK)] * 4,
        hidden, oth, *zboth, k0, v0, k1, v1, k2v3, v2, k3,
        in_specs=[HBM] * 11,
        scratch_shapes=[
            pltpu.VMEM((256, 4 * TOK), F32), pltpu.VMEM((4, 4 * TOK, 2048), BF16),
            pltpu.VMEM((4, 256, 2048), BF16), pltpu.SemaphoreType.DMA((4, 12)),
        ],
        cost=100, vmem=60,
    )
    kv_parts = [kv[0]] + [send(kv[4 - d], x=-d) for d in (1, 2, 3)]

    (chunks,) = move([near, after(far_zl, *kv), near_zh, far_zh], [shape(2048, 256)], cost=0)(chunk_pairs, 4)
    nears = [send(chunks, y=1), send(chunks, y=3)]
    (kv_mine,) = move([after(kv_parts[0], far_zl, near_zh, far_zh), *kv_parts[1:]], [shape(128, 16 * TOK)])(line_pairs, 4)
    kv_other = send(kv_mine, core=1)
    rows_other = send(rows_half, core=1)
    (token,) = call(token_body, [shape(8, BLOCK, dtype=F32)], rows_other, in_specs=[ANY], cost=100)
    *out_other, mine = call(
        attend_body, [shape(4, STEPS, 512)] * 2 + [shape(8, STEPS, 512)],
        rows_half, rows_other, wq_old, kv_mine, kv_other, bounds, wo_old, token,
        in_specs=[HBM] * 5 + [VMEM, HBM, ANY],
        scratch_shapes=[
            pltpu.VMEM((STEPS, 256), BF16), pltpu.VMEM((128, 16 * TOK), BF16), pltpu.VMEM((128, 16 * TOK), BF16),
            pltpu.VMEM((256, WIDE), BF16), pltpu.VMEM((16, STEPS, 512), BF16),
            pltpu.VMEM((8, STEPS, 1024), BF16), pltpu.VMEM((WIDE, 256), BF16),
            pltpu.SemaphoreType.DMA((2,)), pltpu.SemaphoreType.DMA((16,)), pltpu.SemaphoreType.DMA((16,)),
            pltpu.SemaphoreType.DMA((8,)), pltpu.SemaphoreType.DMA((16,)),
        ],
        out_specs=[ANY] * 3,
        vmem=60,
    )
    out_core = [send(o, core=1) for o in out_other]
    (out,) = call(
        add_body, [shape(8, STEPS, 512)], mine, *out_core, in_specs=[HBM] * 3, out_specs=[ANY], vmem=60,
        scratch_shapes=[pltpu.VMEM((8, STEPS, 512), BF16)] * 3
        + [pltpu.SemaphoreType.DMA((16,)), pltpu.SemaphoreType.DMA((8,))],
    )
    summed = swap_all(out, "tp", ZX_GROUPS)

    spots = [jnp.stack([gi // 4, zl, cc, (gi - d) % 4]).astype(jnp.int32) for d in range(4)]
    nears = after(tuple(nears), out)
    on = move(nears, [shape(1024, 256)] * 2, cost=0)(on_pairs, 2)
    last = [send(on[0], y=1), send(on[1], y=3)]

    def sides(*blocks):
        return [b.reshape(-1, 2, 2, 4, 64, 256) for b in blocks]

    done = quantize(sides(*[after(chunks, out)] * 2), spots[0], ())
    done = quantize(sides(nears[0], nears[0]), spots[1], done)
    done = quantize(sides(nears[1], nears[1]), spots[3], done)
    (step_features,) = call(final_body, [shape(STEPS, 512)], summed)
    last = after(tuple(last), step_features)
    done = quantize(sides(*last), spots[2], done)
    quantized = done[0]
    scales = done[1].T
    return (step_features, quantized, scales)


def solution(mesh):
    placed = (
        P(("grp", "tp"), None),
        P("grp", None),
        P(None, "tp"),
        P(None, "tp"),
        P(None, "tp"),
        P("tp", None),
        P(("grp", "tp"), None),
        P(("grp", "tp"), None),
        P(("grp", "tp"), None),
        P(("grp", "tp"), None),
    )
    return jax.shard_map(
        on_device,
        mesh=mesh,
        in_specs=placed,
        out_specs=(P("grp", "tp"), P(None, "tp"), P(None, "tp")),
        check_vma=False,
    )
```

profile of v0, /device:TPU:1, one launch (start us, length us, event | category | flops | bytes accessed | tf_op | source)
XLA Modules:
  0.0 127.1 jit_solution(14843020594138524252)
XLA Ops:
  4.8 1.7 %collective-permute-start.5 = (bf16[96,8192]{1,0:T(8,128)(2,1)}, bf16[96,8192]{1,0:T(8,128)(2,1)}, u32[]{:S(2)}, u32[]{:S(2)}) collective-permute-start(bf16[96,8192]{1,0:T(8,128)(2,1)} %own.1), channel_id=1, source_target_pairs={{0,8},{1,9},{2,10},{3,11},{4,12},{5,13},{6,14},{7,15},{8,0},{9,1},... | collective-permute-start | bytes 4718600 | tf_op jit(solution)/shard_map/ppermute | solution.py:31
  7.7 5.1 %shard_map.121 = bf16[4,192,1024]{2,1,0:T(8,128)(2,1)} custom-call(bf16[64,4096]{1,0:T(8,128)(2,1)} %w_any.1, bf16[64,4096]{1,0:T(8,128)(2,1)} %g_any.1, f32[64,4096]{1,0:T(8,128)} %m_any.1, f32[64,4096]{1,0:T(8,128)} %s_any.1, bf16[96,8192]{1,0:T(8,128)(2,1)} %own.1, bf16[96,8192]{1,0:T(8,128)(2,1)} %copy-done.7, s32[1,128]{1,0:T(1,128)} %bound_ref.3), custom_call_target="tpu_custom_call" | custom-call | flops 99999997952 | tf_op jit(solution)/shard_map/pallas_call | solution.py:85
  12.8 3.6 %all-to-all-start = ((bf16[4,192,1024]{2,1,0:T(8,128)(2,1)}), bf16[4,192,1024]{2,1,0:T(8,128)(2,1)S(1)}, u32[]{:S(2)}, u32[]{:S(2)}) async-start(bf16[4,192,1024]{2,1,0:T(8,128)(2,1)} %shard_map.121), calls=%async_computation | async-start | bytes 3145728 | tf_op jit(solution)/shard_map/all_to_all | solution.py:35
  17.9 2.3 %shard_map.122 = bf16[64,8192]{1,0:T(8,128)(2,1)} custom-call(bf16[32,8192]{1,0:T(8,128)(2,1)} %copy-done.9, bf16[32,8192]{1,0:T(8,128)(2,1)} %bitcast.20), custom_call_target="tpu_custom_call" | custom-call | flops 99999997952 | tf_op jit(solution)/shard_map/pallas_call | solution.py:85
  21.0 1.9 %collective-permute-start.7 = (bf16[32,8192]{1,0:T(8,128)(2,1)S(1)}, bf16[32,8192]{1,0:T(8,128)(2,1)}, u32[]{:S(2)}, u32[]{:S(2)}) collective-permute-start(bf16[32,8192]{1,0:T(8,128)(2,1)S(1)} %bitcast.22), channel_id=1, source_target_pairs={{0,6},{1,7},{2,0},{3,1},{4,2},{5,3},{6,4},{7,5},{8,14},{9,15},{10,... | collective-permute-start | bytes 1572872 | tf_op jit(solution)/shard_map/ppermute | solution.py:31
  22.9 18.1 %collective-permute-done.5.zown = bf16[96,8192]{1,0:T(8,128)(2,1)} collective-permute-done((bf16[96,8192]{1,0:T(8,128)(2,1)}, bf16[96,8192]{1,0:T(8,128)(2,1)}, u32[]{:S(2)}, u32[]{:S(2)}) %collective-permute-start.5) | collective-permute-done | bytes 1572896 | tf_op jit(solution)/shard_map/ppermute | solution.py:31
  43.1 1.5 %collective-permute-start.3 = (bf16[512,256]{1,0:T(8,128)(2,1)S(1)}, bf16[512,256]{1,0:T(8,128)(2,1)S(1)}, u32[]{:S(2)}, u32[]{:S(2)}) collective-permute-start(bf16[512,256]{1,0:T(8,128)(2,1)S(1)} %get-tuple-element.41.mine_any), channel_id=1, source_target_pairs={{0,8},{1,9},{2,10},{3,11},{4,12},{5,13},{6,14},{7,15},{8,0},{9,1},... | collective-permute-start | bytes 786440 | tf_op jit(solution)/shard_map/ppermute | solution.py:31
  44.7 6.6 %collective-permute-done.3.got_any = bf16[512,256]{1,0:T(8,128)(2,1)S(1)} collective-permute-done((bf16[512,256]{1,0:T(8,128)(2,1)S(1)}, bf16[512,256]{1,0:T(8,128)(2,1)S(1)}, u32[]{:S(2)}, u32[]{:S(2)}) %collective-permute-start.3) | collective-permute-done | bytes 262176 | tf_op jit(solution)/shard_map/ppermute | solution.py:31
  56.6 1.5 %collective-permute-start.11 = (bf16[512,256]{1,0:T(8,128)(2,1)S(1)}, bf16[512,256]{1,0:T(8,128)(2,1)S(1)}, u32[]{:S(2)}, u32[]{:S(2)}) collective-permute-start(bf16[512,256]{1,0:T(8,128)(2,1)S(1)} %get-tuple-element.50), channel_id=1, source_target_pairs={{0,8},{1,9},{2,10},{3,11},{4,12},{5,13},{6,14},{7,15},{8,0},{9,1},... | collective-permute-start | bytes 786440 | tf_op jit(solution)/shard_map/ppermute | solution.py:31
  58.1 2.2 %collective-permute-start.13 = (bf16[512,256]{1,0:T(8,128)(2,1)S(1)}, bf16[512,256]{1,0:T(8,128)(2,1)S(1)}, u32[]{:S(2)}, u32[]{:S(2)}) collective-permute-start(bf16[512,256]{1,0:T(8,128)(2,1)S(1)} %get-tuple-element.50), channel_id=1, source_target_pairs={{0,72},{1,73},{2,74},{3,75},{4,76},{5,77},{6,78},{7,79},{8,64},{9,... | collective-permute-start | bytes 786440 | tf_op jit(solution)/shard_map/ppermute | solution.py:31
  60.4 4.2 %all-to-all-start.1 = ((bf16[4,128,1024]{2,1,0:T(8,128)(2,1)}), bf16[4,128,1024]{2,1,0:T(8,128)(2,1)}, u32[]{:S(2)}, u32[]{:S(2)}) async-start(bf16[4,128,1024]{2,1,0:T(8,128)(2,1)} %shard_map.124), calls=%async_computation.1 | async-start | bytes 2097152 | tf_op jit(solution)/shard_map/all_to_all | solution.py:35
  66.6 6.1 %shard_map.125 = (bf16[128,384]{1,0:T(8,128)(2,1)}, bf16[128,384]{1,0:T(8,128)(2,1)}, bf16[128,384]{1,0:T(8,128)(2,1)}, bf16[128,384]{1,0:T(8,128)(2,1)}) custom-call(bf16[96,8192]{1,0:T(8,128)(2,1)} %own.1, bf16[96,8192]{1,0:T(8,128)(2,1)} %copy-done.7, bf16[96,8192]{1,0:T(8,128)(2,1)} %collective-permute-done.5.zown, ...), custom_call_target="tpu_custom_call" | custom-call | flops 99999997952 | tf_op jit(solution)/shard_map/pallas_call | solution.py:85
  72.7 2.6 %collective-permute-start.14 = (bf16[128,384]{1,0:T(8,128)(2,1)}, bf16[128,384]{1,0:T(8,128)(2,1)S(1)}, u32[]{:S(2)}, u32[]{:S(2)}) collective-permute-start(bf16[128,384]{1,0:T(8,128)(2,1)} %get-tuple-element.53), channel_id=1, source_target_pairs={{0,6},{1,7},{2,0},{3,1},{4,2},{5,3},{6,4},{7,5},{8,14},{9,15},{10,... | collective-permute-start | bytes 294920 | tf_op jit(solution)/shard_map/ppermute | solution.py:31
  80.4 2.5 %collective-permute-start.4 = (bf16[4,128,1024]{2,1,0:T(8,128)(2,1)}, bf16[4,128,1024]{2,1,0:T(8,128)(2,1)S(1)}, u32[]{:S(2)}, u32[]{:S(2)}) collective-permute-start(bf16[4,128,1024]{2,1,0:T(8,128)(2,1)} %all-to-all-done.1.rows_any), channel_id=1, source_target_pairs={{0,1},{1,0},{2,3},{3,2},{4,5},{5,4},{6,7},{7,6},{8,9},{9,8},{10,11... | collective-permute-start | bytes 3145736 | tf_op jit(solution)/shard_map/ppermute | solution.py:31
  88.4 8.9 %shard_map.129 = (bf16[4,128,512]{2,1,0:T(8,128)(2,1)}, bf16[4,128,512]{2,1,0:T(8,128)(2,1)}, bf16[8,128,512]{2,1,0:T(8,128)(2,1)}) custom-call(bf16[4,128,1024]{2,1,0:T(8,128)(2,1)} %all-to-all-done.1.rows_any, bf16[4,128,1024]{2,1,0:T(8,128)(2,1)} %copy-done, bf16[8192,256]{1,0:T(8,128)(2,1)} %wq_any.1, bf16[128,1536]{1,0:T(8,128)(2,1)} %copy-done.1, ...), custom_call_target="tpu_custom_call" | custom-call | tf_op jit(solution)/shard_map/pallas_call | solution.py:85
  97.9 1.6 %collective-permute-done.18.got_a = bf16[4,128,512]{2,1,0:T(8,128)(2,1)S(1)} collective-permute-done((bf16[4,128,512]{2,1,0:T(8,128)(2,1)}, bf16[4,128,512]{2,1,0:T(8,128)(2,1)S(1)}, u32[]{:S(2)}, u32[]{:S(2)}) %collective-permute-start.18) | collective-permute-done | bytes 524320 | tf_op jit(solution)/shard_map/ppermute | solution.py:31
  101.1 2.5 %shard_map.130 = bf16[8,128,512]{2,1,0:T(8,128)(2,1)} custom-call(bf16[8,128,512]{2,1,0:T(8,128)(2,1)} %get-tuple-element.56.mine_any, bf16[4,128,512]{2,1,0:T(8,128)(2,1)} %copy-done.4, bf16[4,128,512]{2,1,0:T(8,128)(2,1)} %copy-done.5), custom_call_target="tpu_custom_call" | custom-call | tf_op jit(solution)/shard_map/pallas_call | solution.py:85
  103.6 4.4 %all-to-all-start.2 = ((bf16[8,128,512]{2,1,0:T(8,128)(2,1)}), bf16[8,128,512]{2,1,0:T(8,128)(2,1)S(1)}, u32[]{:S(2)}, u32[]{:S(2)}) async-start(bf16[8,128,512]{2,1,0:T(8,128)(2,1)} %shard_map.130), calls=%async_computation.2 | async-start | bytes 2097152 | tf_op jit(solution)/shard_map/all_to_all | solution.py:35
  110.2 1.7 %collective-permute-start.23 = (bf16[1024,256]{1,0:T(8,128)(2,1)S(1)}, bf16[1024,256]{1,0:T(8,128)(2,1)S(1)}, u32[]{:S(2)}, u32[]{:S(2)}) collective-permute-start(bf16[1024,256]{1,0:T(8,128)(2,1)S(1)} %get-tuple-element.63), channel_id=1, source_target_pairs={{0,48},{1,49},{2,50},{3,51},{4,52},{5,53},{6,54},{7,55},{8,56},{9,... | collective-permute-start | bytes 1572872 | tf_op jit(solution)/shard_map/ppermute | solution.py:31
  112.1 2.8 %shard_map.134 = (bf16[8192,256]{1,0:T(8,128)(2,1)}, f32[2,64]{1,0:T(2,128)S(1)}) custom-call(s32[4]{0:T(128)S(1)} %get-tuple-element.75.at_ref, bf16[2,2,2,4,64,256]{5,4,3,2,1,0:T(8,128)(2,1)} %bitcast.13.refs_0_.refs_1_, bf16[2,2,2,4,64,256]{5,4,3,2,1,0:T(8,128)(2,1)} %bitcast.13.refs_0_.refs_1_), custom_call_target="tpu_custom_call" | custom-call | tf_op jit(solution)/shard_map/pallas_call | solution.py:85
  114.9 2.8 %shard_map.135 = (bf16[8192,256]{1,0:T(8,128)(2,1)}, f32[2,64]{1,0:T(2,128)S(1)}) custom-call(s32[4]{0:T(128)S(1)} %get-tuple-element.77.at_ref, bf16[2,2,2,4,64,256]{5,4,3,2,1,0:T(8,128)(2,1)} %bitcast.11.refs_0_.refs_1_, bf16[2,2,2,4,64,256]{5,4,3,2,1,0:T(8,128)(2,1)} %bitcast.11.refs_0_.refs_1_, ...), custom_call_target="tpu_custom_call", output_to_operand_aliasing={{0}: (3, {})} | custom-call | tf_op jit(solution)/shard_map/pallas_call | solution.py:85
  117.7 2.8 %shard_map.136 = (bf16[8192,256]{1,0:T(8,128)(2,1)}, f32[2,64]{1,0:T(2,128)S(1)}) custom-call(s32[4]{0:T(128)S(1)} %get-tuple-element.78.at_ref, bf16[2,2,2,4,64,256]{5,4,3,2,1,0:T(8,128)(2,1)} %bitcast.9.refs_0_.refs_1_, bf16[2,2,2,4,64,256]{5,4,3,2,1,0:T(8,128)(2,1)} %bitcast.9.refs_0_.refs_1_, ...), custom_call_target="tpu_custom_call", output_to_operand_aliasing={{0}: (3, {})} | custom-call | tf_op jit(solution)/shard_map/pallas_call | solution.py:85
  120.6 3.2 %all-to-all-done.2.got_ref = bf16[8,128,512]{2,1,0:T(8,128)(2,1)S(1)} async-done(((bf16[8,128,512]{2,1,0:T(8,128)(2,1)}), bf16[8,128,512]{2,1,0:T(8,128)(2,1)S(1)}, u32[]{:S(2)}, u32[]{:S(2)}) %all-to-all-start.2) | async-done | bytes 1048608 | tf_op jit(solution)/shard_map/all_to_all | solution.py:35
  124.6 2.4 %shard_map.137 = (bf16[8192,256]{1,0:T(8,128)(2,1)}, f32[2,64]{1,0:T(2,128)}) custom-call(s32[4]{0:T(128)S(1)} %get-tuple-element.79.at_ref, bf16[1,2,2,4,64,256]{5,4,3,2,1,0:T(8,128)(2,1)S(1)} %bitcast.15, bf16[1,2,2,4,64,256]{5,4,3,2,1,0:T(8,128)(2,1)S(1)} %bitcast.16, ...), custom_call_target="tpu_custom_call", output_to_operand_aliasing={{0}: (3, {})} | custom-call | tf_op jit(solution)/shard_map/pallas_call | solution.py:85
  (71 shorter events, 33.0 us)
Async XLA Ops:
  0.6 5.9 %collective-permute-start = (bf16[96,8192]{1,0:T(8,128)(2,1)}, bf16[96,8192]{1,0:T(8,128)(2,1)S(1)}, u32[]{:S(2)}, u32[]{:S(2)}) collective-permute-start(bf16[96,8192]{1,0:T(8,128)(2,1)} %own.1), channel_id=1, source_target_pairs={{0,1},{1,0},{2,3},{3,2},{4,5},{5,4},{6,7},{7,6},{8,9},{9,8},{10,11... | collective-permute-start | bytes 4718600 | tf_op jit(solution)/shard_map/ppermute | solution.py:31
  2.1 14.9 %collective-permute-start.1 = (bf16[32,8192]{1,0:T(8,128)(2,1)}, bf16[32,8192]{1,0:T(8,128)(2,1)S(1)}, u32[]{:S(2)}, u32[]{:S(2)}) collective-permute-start(bf16[32,8192]{1,0:T(8,128)(2,1)} %bitcast.17), channel_id=1, source_target_pairs={{0,2},{1,3},{2,4},{3,5},{4,6},{5,7},{6,0},{7,1},{8,10},{9,11},{10,... | collective-permute-start | bytes 1572872 | tf_op jit(solution)/shard_map/ppermute | solution.py:31
  3.4 13.6 %collective-permute-start.2 = (bf16[32,8192]{1,0:T(8,128)(2,1)}, bf16[32,8192]{1,0:T(8,128)(2,1)}, u32[]{:S(2)}, u32[]{:S(2)}) collective-permute-start(bf16[32,8192]{1,0:T(8,128)(2,1)} %bitcast.18), channel_id=1, source_target_pairs={{0,6},{1,7},{2,0},{3,1},{4,2},{5,3},{6,4},{7,5},{8,14},{9,15},{10,... | collective-permute-start | bytes 1572872 | tf_op jit(solution)/shard_map/ppermute | solution.py:31
  4.8 36.2 %collective-permute-start.5 = (bf16[96,8192]{1,0:T(8,128)(2,1)}, bf16[96,8192]{1,0:T(8,128)(2,1)}, u32[]{:S(2)}, u32[]{:S(2)}) collective-permute-start(bf16[96,8192]{1,0:T(8,128)(2,1)} %own.1), channel_id=1, source_target_pairs={{0,8},{1,9},{2,10},{3,11},{4,12},{5,13},{6,14},{7,15},{8,0},{9,1},... | collective-permute-start | bytes 4718600 | tf_op jit(solution)/shard_map/ppermute | solution.py:31
  12.8 29.4 %all-to-all-start = ((bf16[4,192,1024]{2,1,0:T(8,128)(2,1)}), bf16[4,192,1024]{2,1,0:T(8,128)(2,1)S(1)}, u32[]{:S(2)}, u32[]{:S(2)}) async-start(bf16[4,192,1024]{2,1,0:T(8,128)(2,1)} %shard_map.121), calls=%async_computation | async-start | bytes 3145728 | tf_op jit(solution)/shard_map/all_to_all | solution.py:35
  20.2 45.6 %collective-permute-start.8 = (bf16[64,8192]{1,0:T(8,128)(2,1)}, bf16[64,8192]{1,0:T(8,128)(2,1)}, u32[]{:S(2)}, u32[]{:S(2)}) collective-permute-start(bf16[64,8192]{1,0:T(8,128)(2,1)} %shard_map.122), channel_id=1, source_target_pairs={{0,2},{1,3},{2,4},{3,5},{4,6},{5,7},{6,0},{7,1},{8,10},{9,11},{10,... | collective-permute-start | bytes 3145736 | tf_op jit(solution)/shard_map/ppermute | solution.py:31
  21.0 31.5 %collective-permute-start.7 = (bf16[32,8192]{1,0:T(8,128)(2,1)S(1)}, bf16[32,8192]{1,0:T(8,128)(2,1)}, u32[]{:S(2)}, u32[]{:S(2)}) collective-permute-start(bf16[32,8192]{1,0:T(8,128)(2,1)S(1)} %bitcast.22), channel_id=1, source_target_pairs={{0,6},{1,7},{2,0},{3,1},{4,2},{5,3},{6,4},{7,5},{8,14},{9,15},{10,... | collective-permute-start | bytes 1572872 | tf_op jit(solution)/shard_map/ppermute | solution.py:31
  41.0 23.6 %collective-permute-start.6 = (bf16[96,8192]{1,0:T(8,128)(2,1)}, bf16[96,8192]{1,0:T(8,128)(2,1)}, u32[]{:S(2)}, u32[]{:S(2)}) collective-permute-start(bf16[96,8192]{1,0:T(8,128)(2,1)} %collective-permute-done.5.zown), channel_id=1, source_target_pairs={{0,1},{1,0},{2,3},{3,2},{4,5},{5,4},{6,7},{7,6},{8,9},{9,8},{10,11... | collective-permute-start | bytes 4718600 | tf_op jit(solution)/shard_map/ppermute | solution.py:31
  43.1 8.1 %collective-permute-start.3 = (bf16[512,256]{1,0:T(8,128)(2,1)S(1)}, bf16[512,256]{1,0:T(8,128)(2,1)S(1)}, u32[]{:S(2)}, u32[]{:S(2)}) collective-permute-start(bf16[512,256]{1,0:T(8,128)(2,1)S(1)} %get-tuple-element.41.mine_any), channel_id=1, source_target_pairs={{0,8},{1,9},{2,10},{3,11},{4,12},{5,13},{6,14},{7,15},{8,0},{9,1},... | collective-permute-start | bytes 786440 | tf_op jit(solution)/shard_map/ppermute | solution.py:31
  52.4 13.3 %collective-permute-start.9 = (bf16[32,8192]{1,0:T(8,128)(2,1)}, bf16[32,8192]{1,0:T(8,128)(2,1)S(1)}, u32[]{:S(2)}, u32[]{:S(2)}) collective-permute-start(bf16[32,8192]{1,0:T(8,128)(2,1)} %collective-permute-done.7.v1), channel_id=1, source_target_pairs={{0,6},{1,7},{2,0},{3,1},{4,2},{5,3},{6,4},{7,5},{8,14},{9,15},{10,... | collective-permute-start | bytes 1572872 | tf_op jit(solution)/shard_map/ppermute | solution.py:31
  56.6 19.2 %collective-permute-start.11 = (bf16[512,256]{1,0:T(8,128)(2,1)S(1)}, bf16[512,256]{1,0:T(8,128)(2,1)S(1)}, u32[]{:S(2)}, u32[]{:S(2)}) collective-permute-start(bf16[512,256]{1,0:T(8,128)(2,1)S(1)} %get-tuple-element.50), channel_id=1, source_target_pairs={{0,8},{1,9},{2,10},{3,11},{4,12},{5,13},{6,14},{7,15},{8,0},{9,1},... | collective-permute-start | bytes 786440 | tf_op jit(solution)/shard_map/ppermute | solution.py:31
  58.1 18.3 %collective-permute-start.13 = (bf16[512,256]{1,0:T(8,128)(2,1)S(1)}, bf16[512,256]{1,0:T(8,128)(2,1)S(1)}, u32[]{:S(2)}, u32[]{:S(2)}) collective-permute-start(bf16[512,256]{1,0:T(8,128)(2,1)S(1)} %get-tuple-element.50), channel_id=1, source_target_pairs={{0,72},{1,73},{2,74},{3,75},{4,76},{5,77},{6,78},{7,79},{8,64},{9,... | collective-permute-start | bytes 786440 | tf_op jit(solution)/shard_map/ppermute | solution.py:31
  60.4 20.0 %all-to-all-start.1 = ((bf16[4,128,1024]{2,1,0:T(8,128)(2,1)}), bf16[4,128,1024]{2,1,0:T(8,128)(2,1)}, u32[]{:S(2)}, u32[]{:S(2)}) async-start(bf16[4,128,1024]{2,1,0:T(8,128)(2,1)} %shard_map.124), calls=%async_computation.1 | async-start | bytes 2097152 | tf_op jit(solution)/shard_map/all_to_all | solution.py:35
  64.6 11.8 %collective-permute-start.12 = (bf16[512,256]{1,0:T(8,128)(2,1)S(1)}, bf16[512,256]{1,0:T(8,128)(2,1)S(1)}, u32[]{:S(2)}, u32[]{:S(2)}) collective-permute-start(bf16[512,256]{1,0:T(8,128)(2,1)S(1)} %get-tuple-element.51.refs_0_), channel_id=1, source_target_pairs={{0,64},{1,65},{2,66},{3,67},{4,68},{5,69},{6,70},{7,71},{8,72},{9,... | collective-permute-start | bytes 786440 | tf_op jit(solution)/shard_map/ppermute | solution.py:31
  72.7 7.8 %collective-permute-start.14 = (bf16[128,384]{1,0:T(8,128)(2,1)}, bf16[128,384]{1,0:T(8,128)(2,1)S(1)}, u32[]{:S(2)}, u32[]{:S(2)}) collective-permute-start(bf16[128,384]{1,0:T(8,128)(2,1)} %get-tuple-element.53), channel_id=1, source_target_pairs={{0,6},{1,7},{2,0},{3,1},{4,2},{5,3},{6,4},{7,5},{8,14},{9,15},{10,... | collective-permute-start | bytes 294920 | tf_op jit(solution)/shard_map/ppermute | solution.py:31
  75.3 7.6 %collective-permute-start.15 = (bf16[128,384]{1,0:T(8,128)(2,1)}, bf16[128,384]{1,0:T(8,128)(2,1)S(1)}, u32[]{:S(2)}, u32[]{:S(2)}) collective-permute-start(bf16[128,384]{1,0:T(8,128)(2,1)} %get-tuple-element.54), channel_id=1, source_target_pairs={{0,4},{1,5},{2,6},{3,7},{4,0},{5,1},{6,2},{7,3},{8,12},{9,13},{10,... | collective-permute-start | bytes 294920 | tf_op jit(solution)/shard_map/ppermute | solution.py:31
  75.8 7.7 %collective-permute-start.16 = (bf16[128,384]{1,0:T(8,128)(2,1)}, bf16[128,384]{1,0:T(8,128)(2,1)S(1)}, u32[]{:S(2)}, u32[]{:S(2)}) collective-permute-start(bf16[128,384]{1,0:T(8,128)(2,1)} %get-tuple-element.55), channel_id=1, source_target_pairs={{0,2},{1,3},{2,4},{3,5},{4,6},{5,7},{6,0},{7,1},{8,10},{9,11},{10,... | collective-permute-start | bytes 294920 | tf_op jit(solution)/shard_map/ppermute | solution.py:31
  77.5 30.4 %collective-permute-start.20 = (bf16[2048,256]{1,0:T(8,128)(2,1)}, bf16[2048,256]{1,0:T(8,128)(2,1)}, u32[]{:S(2)}, u32[]{:S(2)}) collective-permute-start(bf16[2048,256]{1,0:T(8,128)(2,1)} %shard_map.132), channel_id=1, source_target_pairs={{0,16},{1,17},{2,18},{3,19},{4,20},{5,21},{6,22},{7,23},{8,24},{9,... | collective-permute-start | bytes 3145736 | tf_op jit(solution)/shard_map/ppermute | solution.py:31
  78.9 29.1 %collective-permute-start.21 = (bf16[2048,256]{1,0:T(8,128)(2,1)}, bf16[2048,256]{1,0:T(8,128)(2,1)}, u32[]{:S(2)}, u32[]{:S(2)}) collective-permute-start(bf16[2048,256]{1,0:T(8,128)(2,1)} %shard_map.132), channel_id=1, source_target_pairs={{0,48},{1,49},{2,50},{3,51},{4,52},{5,53},{6,54},{7,55},{8,56},{9,... | collective-permute-start | bytes 3145736 | tf_op jit(solution)/shard_map/ppermute | solution.py:31
  80.4 5.7 %collective-permute-start.4 = (bf16[4,128,1024]{2,1,0:T(8,128)(2,1)}, bf16[4,128,1024]{2,1,0:T(8,128)(2,1)S(1)}, u32[]{:S(2)}, u32[]{:S(2)}) collective-permute-start(bf16[4,128,1024]{2,1,0:T(8,128)(2,1)} %all-to-all-done.1.rows_any), channel_id=1, source_target_pairs={{0,1},{1,0},{2,3},{3,2},{4,5},{5,4},{6,7},{7,6},{8,9},{9,8},{10,11... | collective-permute-start | bytes 3145736 | tf_op jit(solution)/shard_map/ppermute | solution.py:31
  84.6 3.1 %collective-permute-start.17 = (bf16[128,1536]{1,0:T(8,128)(2,1)S(1)}, bf16[128,1536]{1,0:T(8,128)(2,1)S(1)}, u32[]{:S(2)}, u32[]{:S(2)}) collective-permute-start(bf16[128,1536]{1,0:T(8,128)(2,1)S(1)} %shard_map.127.half_any), channel_id=1, source_target_pairs={{0,1},{1,0},{2,3},{3,2},{4,5},{5,4},{6,7},{7,6},{8,9},{9,8},{10,11... | collective-permute-start | bytes 1179656 | tf_op jit(solution)/shard_map/ppermute | solution.py:31
  103.6 20.2 %all-to-all-start.2 = ((bf16[8,128,512]{2,1,0:T(8,128)(2,1)}), bf16[8,128,512]{2,1,0:T(8,128)(2,1)S(1)}, u32[]{:S(2)}, u32[]{:S(2)}) async-start(bf16[8,128,512]{2,1,0:T(8,128)(2,1)} %shard_map.130), calls=%async_computation.2 | async-start | bytes 2097152 | tf_op jit(solution)/shard_map/all_to_all | solution.py:35
  109.2 15.4 %collective-permute-start.22 = (bf16[1024,256]{1,0:T(8,128)(2,1)S(1)}, bf16[1024,256]{1,0:T(8,128)(2,1)S(1)}, u32[]{:S(2)}, u32[]{:S(2)}) collective-permute-start(bf16[1024,256]{1,0:T(8,128)(2,1)S(1)} %get-tuple-element.62), channel_id=1, source_target_pairs={{0,16},{1,17},{2,18},{3,19},{4,20},{5,21},{6,22},{7,23},{8,24},{9,... | collective-permute-start | bytes 1572872 | tf_op jit(solution)/shard_map/ppermute | solution.py:31
  110.2 14.4 %collective-permute-start.23 = (bf16[1024,256]{1,0:T(8,128)(2,1)S(1)}, bf16[1024,256]{1,0:T(8,128)(2,1)S(1)}, u32[]{:S(2)}, u32[]{:S(2)}) collective-permute-start(bf16[1024,256]{1,0:T(8,128)(2,1)S(1)} %get-tuple-element.63), channel_id=1, source_target_pairs={{0,48},{1,49},{2,50},{3,51},{4,52},{5,53},{6,54},{7,55},{8,56},{9,... | collective-permute-start | bytes 1572872 | tf_op jit(solution)/shard_map/ppermute | solution.py:31
  (14 other events, 19.2 us)
where the time goes:
time: 128 us; the launch traced here: 127 us
  starting transfers between devices  44.8 us (35%)
  Pallas kernels  41.6 us (32%)
  waiting for transfers between devices  32.8 us (26%)
  local copies, waits for them, and re-layouts  6.77 us (5%)
    pallas_call x17, Pallas kernels, call(): pl.pallas_call(body, out_shape=outs, cost_estimate=pl.CostEstimate(flops=...  41.6 us
    ppermute x24, starting transfers between devices, send(): return lax.ppermute(value, AXES, pairs)  32.6 us
    ppermute x24, waiting for transfers between devices, send(): return lax.ppermute(value, AXES, pairs)  29.6 us
    all_to_all x3, starting transfers between devices, swap_all(): lax.all_to_all(value, axis, split_axis=0, concat_axis=0, axis_index_group...  12.2 us
    unnamed x22, local copies, waits for them, and re-layouts  6.77 us
    all_to_all x3, waiting for transfers between devices, swap_all(): lax.all_to_all(value, axis, split_axis=0, concat_axis=0, axis_index_group...  3.25 us
  transfers between devices with their start and end apart: 27, of which 8 were waited for; matrix products, arithmetic and copies ran while one was open for 0% of the time, Pallas kernels for 31%

commit v1 on v0

--- a/solution.py
+++ b/solution.py
@@ -362,12 +362,12 @@
         in_specs=[HBM] * 6 + [VMEM],
         scratch_shapes=[pltpu.VMEM((64, 4096), BF16)] * 2 + [pltpu.VMEM((64, 4096), F32)] * 2
         + [pltpu.VMEM((TOK, 4096), BF16)] * 2 + [pltpu.SemaphoreType.DMA((8,))],
-        cost=100, vmem=60,
+        cost=4, vmem=60,
     )
     got = swap_all(parts, "tp", X_GROUPS)
     v0 = wv_old.T
     (joined,) = call(
-        join_body, [shape(64, WIDE)], after(k3, k1, parts), v0, in_specs=[HBM] * 2, vmem=60, cost=100,
+        join_body, [shape(64, WIDE)], after(k3, k1, parts), v0, in_specs=[HBM] * 2, vmem=60, cost=8,
         scratch_shapes=[pltpu.SemaphoreType.DMA((2,))],
     )
     k2v3 = send(joined, x=1)

time: 128 us -> 126 us (0.984)
  waiting for transfers between devices: 32.8 us -> 30.7 us
    ppermute x24, waiting for transfers between devices: 29.6 us -> 27.4 us  [send(): return lax.ppermute(value, AXES, pairs)]
where the time goes in v1:
time: 126 us
  starting transfers between devices  45.5 us (36%)
  Pallas kernels  41.6 us (33%)
  waiting for transfers between devices  30.7 us (24%)
  local copies, waits for them, and re-layouts  6.77 us (5%)
    pallas_call x17, Pallas kernels, call(): pl.pallas_call(body, out_shape=outs, cost_estimate=pl.CostEstimate(flops=...  41.6 us
    ppermute x24, starting transfers between devices, send(): return lax.ppermute(value, AXES, pairs)  33.3 us
    ppermute x24, waiting for transfers between devices, send(): return lax.ppermute(value, AXES, pairs)  27.4 us
    all_to_all x3, starting transfers between devices, swap_all(): lax.all_to_all(value, axis, split_axis=0, concat_axis=0, axis_index_group...  12.2 us
    unnamed x22, local copies, waits for them, and re-layouts  6.77 us
    all_to_all x3, waiting for transfers between devices, swap_all(): lax.all_to_all(value, axis, split_axis=0, concat_axis=0, axis_index_group...  3.25 us
  transfers between devices with their start and end apart: 27, of which 8 were waited for; matrix products, arithmetic and copies ran while one was open for 0% of the time, Pallas kernels for 31%

profile of v1, /device:TPU:1, one launch (start us, length us, event | category | flops | bytes accessed | tf_op | source)
XLA Modules:
  0.0 125.7 jit_solution(12793337253316282896)
XLA Ops:
  2.1 1.7 %collective-permute-start.5 = (bf16[96,8192]{1,0:T(8,128)(2,1)}, bf16[96,8192]{1,0:T(8,128)(2,1)}, u32[]{:S(2)}, u32[]{:S(2)}) collective-permute-start(bf16[96,8192]{1,0:T(8,128)(2,1)} %own.1), channel_id=1, source_target_pairs={{0,8},{1,9},{2,10},{3,11},{4,12},{5,13},{6,14},{7,15},{8,0},{9,1},... | collective-permute-start | bytes 4718600 | tf_op jit(solution)/shard_map/ppermute | solution.py:31
  7.7 5.1 %shard_map.121 = bf16[4,192,1024]{2,1,0:T(8,128)(2,1)} custom-call(bf16[64,4096]{1,0:T(8,128)(2,1)} %w_any.1, bf16[64,4096]{1,0:T(8,128)(2,1)} %g_any.1, f32[64,4096]{1,0:T(8,128)} %m_any.1, f32[64,4096]{1,0:T(8,128)} %s_any.1, bf16[96,8192]{1,0:T(8,128)(2,1)} %own.1, bf16[96,8192]{1,0:T(8,128)(2,1)} %copy-done.7, s32[1,128]{1,0:T(1,128)} %bound_ref.3), custom_call_target="tpu_custom_call" | custom-call | flops 4000000000 | tf_op jit(solution)/shard_map/pallas_call | solution.py:85
  12.8 3.6 %all-to-all-start = ((bf16[4,192,1024]{2,1,0:T(8,128)(2,1)}), bf16[4,192,1024]{2,1,0:T(8,128)(2,1)S(1)}, u32[]{:S(2)}, u32[]{:S(2)}) async-start(bf16[4,192,1024]{2,1,0:T(8,128)(2,1)} %shard_map.121), calls=%async_computation | async-start | bytes 3145728 | tf_op jit(solution)/shard_map/all_to_all | solution.py:35
  16.4 2.1 %collective-permute-done.1.top_any.k3 = bf16[32,8192]{1,0:T(8,128)(2,1)S(1)} collective-permute-done((bf16[32,8192]{1,0:T(8,128)(2,1)}, bf16[32,8192]{1,0:T(8,128)(2,1)S(1)}, u32[]{:S(2)}, u32[]{:S(2)}) %collective-permute-start.1) | collective-permute-done | bytes 524320 | tf_op jit(solution)/shard_map/ppermute | solution.py:31
  19.3 2.3 %shard_map.122 = bf16[64,8192]{1,0:T(8,128)(2,1)} custom-call(bf16[32,8192]{1,0:T(8,128)(2,1)} %copy-done.9, bf16[32,8192]{1,0:T(8,128)(2,1)} %bitcast.20), custom_call_target="tpu_custom_call" | custom-call | flops 8000000000 | tf_op jit(solution)/shard_map/pallas_call | solution.py:85
  21.8 2.5 %collective-permute-start.7 = (bf16[32,8192]{1,0:T(8,128)(2,1)S(1)}, bf16[32,8192]{1,0:T(8,128)(2,1)}, u32[]{:S(2)}, u32[]{:S(2)}) collective-permute-start(bf16[32,8192]{1,0:T(8,128)(2,1)S(1)} %bitcast.22), channel_id=1, source_target_pairs={{0,6},{1,7},{2,0},{3,1},{4,2},{5,3},{6,4},{7,5},{8,14},{9,15},{10,... | collective-permute-start | bytes 1572872 | tf_op jit(solution)/shard_map/ppermute | solution.py:31
  24.3 14.5 %collective-permute-done.5.zown = bf16[96,8192]{1,0:T(8,128)(2,1)} collective-permute-done((bf16[96,8192]{1,0:T(8,128)(2,1)}, bf16[96,8192]{1,0:T(8,128)(2,1)}, u32[]{:S(2)}, u32[]{:S(2)}) %collective-permute-start.5) | collective-permute-done | bytes 1572896 | tf_op jit(solution)/shard_map/ppermute | solution.py:31
  42.0 6.6 %collective-permute-done.3.got_any = bf16[512,256]{1,0:T(8,128)(2,1)S(1)} collective-permute-done((bf16[512,256]{1,0:T(8,128)(2,1)S(1)}, bf16[512,256]{1,0:T(8,128)(2,1)S(1)}, u32[]{:S(2)}, u32[]{:S(2)}) %collective-permute-start.3) | collective-permute-done | bytes 262176 | tf_op jit(solution)/shard_map/ppermute | solution.py:31
  49.8 2.5 %collective-permute-start.9 = (bf16[32,8192]{1,0:T(8,128)(2,1)}, bf16[32,8192]{1,0:T(8,128)(2,1)S(1)}, u32[]{:S(2)}, u32[]{:S(2)}) collective-permute-start(bf16[32,8192]{1,0:T(8,128)(2,1)} %collective-permute-done.7.v1), channel_id=1, source_target_pairs={{0,6},{1,7},{2,0},{3,1},{4,2},{5,3},{6,4},{7,5},{8,14},{9,15},{10,... | collective-permute-start | bytes 1572872 | tf_op jit(solution)/shard_map/ppermute | solution.py:31
  56.7 2.2 %collective-permute-start.13 = (bf16[512,256]{1,0:T(8,128)(2,1)S(1)}, bf16[512,256]{1,0:T(8,128)(2,1)S(1)}, u32[]{:S(2)}, u32[]{:S(2)}) collective-permute-start(bf16[512,256]{1,0:T(8,128)(2,1)S(1)} %get-tuple-element.50), channel_id=1, source_target_pairs={{0,72},{1,73},{2,74},{3,75},{4,76},{5,77},{6,78},{7,79},{8,64},{9,... | collective-permute-start | bytes 786440 | tf_op jit(solution)/shard_map/ppermute | solution.py:31
  58.9 4.2 %all-to-all-start.1 = ((bf16[4,128,1024]{2,1,0:T(8,128)(2,1)}), bf16[4,128,1024]{2,1,0:T(8,128)(2,1)}, u32[]{:S(2)}, u32[]{:S(2)}) async-start(bf16[4,128,1024]{2,1,0:T(8,128)(2,1)} %shard_map.124), calls=%async_computation.1 | async-start | bytes 2097152 | tf_op jit(solution)/shard_map/all_to_all | solution.py:35
  65.1 6.0 %shard_map.125 = (bf16[128,384]{1,0:T(8,128)(2,1)}, bf16[128,384]{1,0:T(8,128)(2,1)}, bf16[128,384]{1,0:T(8,128)(2,1)}, bf16[128,384]{1,0:T(8,128)(2,1)}) custom-call(bf16[96,8192]{1,0:T(8,128)(2,1)} %own.1, bf16[96,8192]{1,0:T(8,128)(2,1)} %copy-done.7, bf16[96,8192]{1,0:T(8,128)(2,1)} %collective-permute-done.5.zown, ...), custom_call_target="tpu_custom_call" | custom-call | flops 99999997952 | tf_op jit(solution)/shard_map/pallas_call | solution.py:85
  71.2 2.6 %collective-permute-start.14 = (bf16[128,384]{1,0:T(8,128)(2,1)}, bf16[128,384]{1,0:T(8,128)(2,1)S(1)}, u32[]{:S(2)}, u32[]{:S(2)}) collective-permute-start(bf16[128,384]{1,0:T(8,128)(2,1)} %get-tuple-element.53), channel_id=1, source_target_pairs={{0,6},{1,7},{2,0},{3,1},{4,2},{5,3},{6,4},{7,5},{8,14},{9,15},{10,... | collective-permute-start | bytes 294920 | tf_op jit(solution)/shard_map/ppermute | solution.py:31
  79.0 2.5 %collective-permute-start.4 = (bf16[4,128,1024]{2,1,0:T(8,128)(2,1)}, bf16[4,128,1024]{2,1,0:T(8,128)(2,1)S(1)}, u32[]{:S(2)}, u32[]{:S(2)}) collective-permute-start(bf16[4,128,1024]{2,1,0:T(8,128)(2,1)} %all-to-all-done.1.rows_any), channel_id=1, source_target_pairs={{0,1},{1,0},{2,3},{3,2},{4,5},{5,4},{6,7},{7,6},{8,9},{9,8},{10,11... | collective-permute-start | bytes 3145736 | tf_op jit(solution)/shard_map/ppermute | solution.py:31
  87.0 8.9 %shard_map.129 = (bf16[4,128,512]{2,1,0:T(8,128)(2,1)}, bf16[4,128,512]{2,1,0:T(8,128)(2,1)}, bf16[8,128,512]{2,1,0:T(8,128)(2,1)}) custom-call(bf16[4,128,1024]{2,1,0:T(8,128)(2,1)} %all-to-all-done.1.rows_any, bf16[4,128,1024]{2,1,0:T(8,128)(2,1)} %copy-done, bf16[8192,256]{1,0:T(8,128)(2,1)} %wq_any.1, bf16[128,1536]{1,0:T(8,128)(2,1)} %copy-done.1, ...), custom_call_target="tpu_custom_call" | custom-call | tf_op jit(solution)/shard_map/pallas_call | solution.py:85
  96.5 1.6 %collective-permute-done.18.got_a = bf16[4,128,512]{2,1,0:T(8,128)(2,1)S(1)} collective-permute-done((bf16[4,128,512]{2,1,0:T(8,128)(2,1)}, bf16[4,128,512]{2,1,0:T(8,128)(2,1)S(1)}, u32[]{:S(2)}, u32[]{:S(2)}) %collective-permute-start.18) | collective-permute-done | bytes 524320 | tf_op jit(solution)/shard_map/ppermute | solution.py:31
  99.6 2.5 %shard_map.130 = bf16[8,128,512]{2,1,0:T(8,128)(2,1)} custom-call(bf16[8,128,512]{2,1,0:T(8,128)(2,1)} %get-tuple-element.56.mine_any, bf16[4,128,512]{2,1,0:T(8,128)(2,1)} %copy-done.4, bf16[4,128,512]{2,1,0:T(8,128)(2,1)} %copy-done.5), custom_call_target="tpu_custom_call" | custom-call | tf_op jit(solution)/shard_map/pallas_call | solution.py:85
  102.1 4.4 %all-to-all-start.2 = ((bf16[8,128,512]{2,1,0:T(8,128)(2,1)}), bf16[8,128,512]{2,1,0:T(8,128)(2,1)S(1)}, u32[]{:S(2)}, u32[]{:S(2)}) async-start(bf16[8,128,512]{2,1,0:T(8,128)(2,1)} %shard_map.130), calls=%async_computation.2 | async-start | bytes 2097152 | tf_op jit(solution)/shard_map/all_to_all | solution.py:35
  108.7 1.7 %collective-permute-start.23 = (bf16[1024,256]{1,0:T(8,128)(2,1)S(1)}, bf16[1024,256]{1,0:T(8,128)(2,1)S(1)}, u32[]{:S(2)}, u32[]{:S(2)}) collective-permute-start(bf16[1024,256]{1,0:T(8,128)(2,1)S(1)} %get-tuple-element.63), channel_id=1, source_target_pairs={{0,48},{1,49},{2,50},{3,51},{4,52},{5,53},{6,54},{7,55},{8,56},{9,... | collective-permute-start | bytes 1572872 | tf_op jit(solution)/shard_map/ppermute | solution.py:31
  110.6 2.8 %shard_map.134 = (bf16[8192,256]{1,0:T(8,128)(2,1)}, f32[2,64]{1,0:T(2,128)S(1)}) custom-call(s32[4]{0:T(128)S(1)} %get-tuple-element.75.at_ref, bf16[2,2,2,4,64,256]{5,4,3,2,1,0:T(8,128)(2,1)} %bitcast.13.refs_0_.refs_1_, bf16[2,2,2,4,64,256]{5,4,3,2,1,0:T(8,128)(2,1)} %bitcast.13.refs_0_.refs_1_), custom_call_target="tpu_custom_call" | custom-call | tf_op jit(solution)/shard_map/pallas_call | solution.py:85
  113.5 2.8 %shard_map.135 = (bf16[8192,256]{1,0:T(8,128)(2,1)}, f32[2,64]{1,0:T(2,128)S(1)}) custom-call(s32[4]{0:T(128)S(1)} %get-tuple-element.77.at_ref, bf16[2,2,2,4,64,256]{5,4,3,2,1,0:T(8,128)(2,1)} %bitcast.11.refs_0_.refs_1_, bf16[2,2,2,4,64,256]{5,4,3,2,1,0:T(8,128)(2,1)} %bitcast.11.refs_0_.refs_1_, ...), custom_call_target="tpu_custom_call", output_to_operand_aliasing={{0}: (3, {})} | custom-call | tf_op jit(solution)/shard_map/pallas_call | solution.py:85
  116.3 2.8 %shard_map.136 = (bf16[8192,256]{1,0:T(8,128)(2,1)}, f32[2,64]{1,0:T(2,128)S(1)}) custom-call(s32[4]{0:T(128)S(1)} %get-tuple-element.78.at_ref, bf16[2,2,2,4,64,256]{5,4,3,2,1,0:T(8,128)(2,1)} %bitcast.9.refs_0_.refs_1_, bf16[2,2,2,4,64,256]{5,4,3,2,1,0:T(8,128)(2,1)} %bitcast.9.refs_0_.refs_1_, ...), custom_call_target="tpu_custom_call", output_to_operand_aliasing={{0}: (3, {})} | custom-call | tf_op jit(solution)/shard_map/pallas_call | solution.py:85
  119.1 3.2 %all-to-all-done.2.got_ref = bf16[8,128,512]{2,1,0:T(8,128)(2,1)S(1)} async-done(((bf16[8,128,512]{2,1,0:T(8,128)(2,1)}), bf16[8,128,512]{2,1,0:T(8,128)(2,1)S(1)}, u32[]{:S(2)}, u32[]{:S(2)}) %all-to-all-start.2) | async-done | bytes 1048608 | tf_op jit(solution)/shard_map/all_to_all | solution.py:35
  123.1 2.4 %shard_map.137 = (bf16[8192,256]{1,0:T(8,128)(2,1)}, f32[2,64]{1,0:T(2,128)}) custom-call(s32[4]{0:T(128)S(1)} %get-tuple-element.79.at_ref, bf16[1,2,2,4,64,256]{5,4,3,2,1,0:T(8,128)(2,1)S(1)} %bitcast.15, bf16[1,2,2,4,64,256]{5,4,3,2,1,0:T(8,128)(2,1)S(1)} %bitcast.16, ...), custom_call_target="tpu_custom_call", output_to_operand_aliasing={{0}: (3, {})} | custom-call | tf_op jit(solution)/shard_map/pallas_call | solution.py:85
  (71 shorter events, 33.0 us)
Async XLA Ops:
  0.6 5.9 %collective-permute-start = (bf16[96,8192]{1,0:T(8,128)(2,1)}, bf16[96,8192]{1,0:T(8,128)(2,1)S(1)}, u32[]{:S(2)}, u32[]{:S(2)}) collective-permute-start(bf16[96,8192]{1,0:T(8,128)(2,1)} %own.1), channel_id=1, source_target_pairs={{0,1},{1,0},{2,3},{3,2},{4,5},{5,4},{6,7},{7,6},{8,9},{9,8},{10,11... | collective-permute-start | bytes 4718600 | tf_op jit(solution)/shard_map/ppermute | solution.py:31
  2.1 36.7 %collective-permute-start.5 = (bf16[96,8192]{1,0:T(8,128)(2,1)}, bf16[96,8192]{1,0:T(8,128)(2,1)}, u32[]{:S(2)}, u32[]{:S(2)}) collective-permute-start(bf16[96,8192]{1,0:T(8,128)(2,1)} %own.1), channel_id=1, source_target_pairs={{0,8},{1,9},{2,10},{3,11},{4,12},{5,13},{6,14},{7,15},{8,0},{9,1},... | collective-permute-start | bytes 4718600 | tf_op jit(solution)/shard_map/ppermute | solution.py:31
  3.9 14.6 %collective-permute-start.1 = (bf16[32,8192]{1,0:T(8,128)(2,1)}, bf16[32,8192]{1,0:T(8,128)(2,1)S(1)}, u32[]{:S(2)}, u32[]{:S(2)}) collective-permute-start(bf16[32,8192]{1,0:T(8,128)(2,1)} %bitcast.17), channel_id=1, source_target_pairs={{0,2},{1,3},{2,4},{3,5},{4,6},{5,7},{6,0},{7,1},{8,10},{9,11},{10,... | collective-permute-start | bytes 1572872 | tf_op jit(solution)/shard_map/ppermute | solution.py:31
  5.1 13.4 %collective-permute-start.2 = (bf16[32,8192]{1,0:T(8,128)(2,1)}, bf16[32,8192]{1,0:T(8,128)(2,1)}, u32[]{:S(2)}, u32[]{:S(2)}) collective-permute-start(bf16[32,8192]{1,0:T(8,128)(2,1)} %bitcast.18), channel_id=1, source_target_pairs={{0,6},{1,7},{2,0},{3,1},{4,2},{5,3},{6,4},{7,5},{8,14},{9,15},{10,... | collective-permute-start | bytes 1572872 | tf_op jit(solution)/shard_map/ppermute | solution.py:31
  12.8 26.7 %all-to-all-start = ((bf16[4,192,1024]{2,1,0:T(8,128)(2,1)}), bf16[4,192,1024]{2,1,0:T(8,128)(2,1)S(1)}, u32[]{:S(2)}, u32[]{:S(2)}) async-start(bf16[4,192,1024]{2,1,0:T(8,128)(2,1)} %shard_map.121), calls=%async_computation | async-start | bytes 3145728 | tf_op jit(solution)/shard_map/all_to_all | solution.py:35
  21.5 42.8 %collective-permute-start.8 = (bf16[64,8192]{1,0:T(8,128)(2,1)}, bf16[64,8192]{1,0:T(8,128)(2,1)}, u32[]{:S(2)}, u32[]{:S(2)}) collective-permute-start(bf16[64,8192]{1,0:T(8,128)(2,1)} %shard_map.122), channel_id=1, source_target_pairs={{0,2},{1,3},{2,4},{3,5},{4,6},{5,7},{6,0},{7,1},{8,10},{9,11},{10,... | collective-permute-start | bytes 3145736 | tf_op jit(solution)/shard_map/ppermute | solution.py:31
  21.8 28.0 %collective-permute-start.7 = (bf16[32,8192]{1,0:T(8,128)(2,1)S(1)}, bf16[32,8192]{1,0:T(8,128)(2,1)}, u32[]{:S(2)}, u32[]{:S(2)}) collective-permute-start(bf16[32,8192]{1,0:T(8,128)(2,1)S(1)} %bitcast.22), channel_id=1, source_target_pairs={{0,6},{1,7},{2,0},{3,1},{4,2},{5,3},{6,4},{7,5},{8,14},{9,15},{10,... | collective-permute-start | bytes 1572872 | tf_op jit(solution)/shard_map/ppermute | solution.py:31
  38.8 24.4 %collective-permute-start.6 = (bf16[96,8192]{1,0:T(8,128)(2,1)}, bf16[96,8192]{1,0:T(8,128)(2,1)}, u32[]{:S(2)}, u32[]{:S(2)}) collective-permute-start(bf16[96,8192]{1,0:T(8,128)(2,1)} %collective-permute-done.5.zown), channel_id=1, source_target_pairs={{0,1},{1,0},{2,3},{3,2},{4,5},{5,4},{6,7},{7,6},{8,9},{9,8},{10,11... | collective-permute-start | bytes 4718600 | tf_op jit(solution)/shard_map/ppermute | solution.py:31
  40.4 8.2 %collective-permute-start.3 = (bf16[512,256]{1,0:T(8,128)(2,1)S(1)}, bf16[512,256]{1,0:T(8,128)(2,1)S(1)}, u32[]{:S(2)}, u32[]{:S(2)}) collective-permute-start(bf16[512,256]{1,0:T(8,128)(2,1)S(1)} %get-tuple-element.41.mine_any), channel_id=1, source_target_pairs={{0,8},{1,9},{2,10},{3,11},{4,12},{5,13},{6,14},{7,15},{8,0},{9,1},... | collective-permute-start | bytes 786440 | tf_op jit(solution)/shard_map/ppermute | solution.py:31
  49.8 14.5 %collective-permute-start.9 = (bf16[32,8192]{1,0:T(8,128)(2,1)}, bf16[32,8192]{1,0:T(8,128)(2,1)S(1)}, u32[]{:S(2)}, u32[]{:S(2)}) collective-permute-start(bf16[32,8192]{1,0:T(8,128)(2,1)} %collective-permute-done.7.v1), channel_id=1, source_target_pairs={{0,6},{1,7},{2,0},{3,1},{4,2},{5,3},{6,4},{7,5},{8,14},{9,15},{10,... | collective-permute-start | bytes 1572872 | tf_op jit(solution)/shard_map/ppermute | solution.py:31
  55.1 19.2 %collective-permute-start.11 = (bf16[512,256]{1,0:T(8,128)(2,1)S(1)}, bf16[512,256]{1,0:T(8,128)(2,1)S(1)}, u32[]{:S(2)}, u32[]{:S(2)}) collective-permute-start(bf16[512,256]{1,0:T(8,128)(2,1)S(1)} %get-tuple-element.50), channel_id=1, source_target_pairs={{0,8},{1,9},{2,10},{3,11},{4,12},{5,13},{6,14},{7,15},{8,0},{9,1},... | collective-permute-start | bytes 786440 | tf_op jit(solution)/shard_map/ppermute | solution.py:31
  56.7 18.3 %collective-permute-start.13 = (bf16[512,256]{1,0:T(8,128)(2,1)S(1)}, bf16[512,256]{1,0:T(8,128)(2,1)S(1)}, u32[]{:S(2)}, u32[]{:S(2)}) collective-permute-start(bf16[512,256]{1,0:T(8,128)(2,1)S(1)} %get-tuple-element.50), channel_id=1, source_target_pairs={{0,72},{1,73},{2,74},{3,75},{4,76},{5,77},{6,78},{7,79},{8,64},{9,... | collective-permute-start | bytes 786440 | tf_op jit(solution)/shard_map/ppermute | solution.py:31
  58.9 20.0 %all-to-all-start.1 = ((bf16[4,128,1024]{2,1,0:T(8,128)(2,1)}), bf16[4,128,1024]{2,1,0:T(8,128)(2,1)}, u32[]{:S(2)}, u32[]{:S(2)}) async-start(bf16[4,128,1024]{2,1,0:T(8,128)(2,1)} %shard_map.124), calls=%async_computation.1 | async-start | bytes 2097152 | tf_op jit(solution)/shard_map/all_to_all | solution.py:35
  63.2 11.8 %collective-permute-start.12 = (bf16[512,256]{1,0:T(8,128)(2,1)S(1)}, bf16[512,256]{1,0:T(8,128)(2,1)S(1)}, u32[]{:S(2)}, u32[]{:S(2)}) collective-permute-start(bf16[512,256]{1,0:T(8,128)(2,1)S(1)} %get-tuple-element.51.refs_0_), channel_id=1, source_target_pairs={{0,64},{1,65},{2,66},{3,67},{4,68},{5,69},{6,70},{7,71},{8,72},{9,... | collective-permute-start | bytes 786440 | tf_op jit(solution)/shard_map/ppermute | solution.py:31
  71.2 7.8 %collective-permute-start.14 = (bf16[128,384]{1,0:T(8,128)(2,1)}, bf16[128,384]{1,0:T(8,128)(2,1)S(1)}, u32[]{:S(2)}, u32[]{:S(2)}) collective-permute-start(bf16[128,384]{1,0:T(8,128)(2,1)} %get-tuple-element.53), channel_id=1, source_target_pairs={{0,6},{1,7},{2,0},{3,1},{4,2},{5,3},{6,4},{7,5},{8,14},{9,15},{10,... | collective-permute-start | bytes 294920 | tf_op jit(solution)/shard_map/ppermute | solution.py:31
  73.8 7.6 %collective-permute-start.15 = (bf16[128,384]{1,0:T(8,128)(2,1)}, bf16[128,384]{1,0:T(8,128)(2,1)S(1)}, u32[]{:S(2)}, u32[]{:S(2)}) collective-permute-start(bf16[128,384]{1,0:T(8,128)(2,1)} %get-tuple-element.54), channel_id=1, source_target_pairs={{0,4},{1,5},{2,6},{3,7},{4,0},{5,1},{6,2},{7,3},{8,12},{9,13},{10,... | collective-permute-start | bytes 294920 | tf_op jit(solution)/shard_map/ppermute | solution.py:31
  74.4 7.7 %collective-permute-start.16 = (bf16[128,384]{1,0:T(8,128)(2,1)}, bf16[128,384]{1,0:T(8,128)(2,1)S(1)}, u32[]{:S(2)}, u32[]{:S(2)}) collective-permute-start(bf16[128,384]{1,0:T(8,128)(2,1)} %get-tuple-element.55), channel_id=1, source_target_pairs={{0,2},{1,3},{2,4},{3,5},{4,6},{5,7},{6,0},{7,1},{8,10},{9,11},{10,... | collective-permute-start | bytes 294920 | tf_op jit(solution)/shard_map/ppermute | solution.py:31
  76.1 30.4 %collective-permute-start.20 = (bf16[2048,256]{1,0:T(8,128)(2,1)}, bf16[2048,256]{1,0:T(8,128)(2,1)}, u32[]{:S(2)}, u32[]{:S(2)}) collective-permute-start(bf16[2048,256]{1,0:T(8,128)(2,1)} %shard_map.132), channel_id=1, source_target_pairs={{0,16},{1,17},{2,18},{3,19},{4,20},{5,21},{6,22},{7,23},{8,24},{9,... | collective-permute-start | bytes 3145736 | tf_op jit(solution)/shard_map/ppermute | solution.py:31
  77.4 29.1 %collective-permute-start.21 = (bf16[2048,256]{1,0:T(8,128)(2,1)}, bf16[2048,256]{1,0:T(8,128)(2,1)}, u32[]{:S(2)}, u32[]{:S(2)}) collective-permute-start(bf16[2048,256]{1,0:T(8,128)(2,1)} %shard_map.132), channel_id=1, source_target_pairs={{0,48},{1,49},{2,50},{3,51},{4,52},{5,53},{6,54},{7,55},{8,56},{9,... | collective-permute-start | bytes 3145736 | tf_op jit(solution)/shard_map/ppermute | solution.py:31
  79.0 5.7 %collective-permute-start.4 = (bf16[4,128,1024]{2,1,0:T(8,128)(2,1)}, bf16[4,128,1024]{2,1,0:T(8,128)(2,1)S(1)}, u32[]{:S(2)}, u32[]{:S(2)}) collective-permute-start(bf16[4,128,1024]{2,1,0:T(8,128)(2,1)} %all-to-all-done.1.rows_any), channel_id=1, source_target_pairs={{0,1},{1,0},{2,3},{3,2},{4,5},{5,4},{6,7},{7,6},{8,9},{9,8},{10,11... | collective-permute-start | bytes 3145736 | tf_op jit(solution)/shard_map/ppermute | solution.py:31
  83.1 3.1 %collective-permute-start.17 = (bf16[128,1536]{1,0:T(8,128)(2,1)S(1)}, bf16[128,1536]{1,0:T(8,128)(2,1)S(1)}, u32[]{:S(2)}, u32[]{:S(2)}) collective-permute-start(bf16[128,1536]{1,0:T(8,128)(2,1)S(1)} %shard_map.127.half_any), channel_id=1, source_target_pairs={{0,1},{1,0},{2,3},{3,2},{4,5},{5,4},{6,7},{7,6},{8,9},{9,8},{10,11... | collective-permute-start | bytes 1179656 | tf_op jit(solution)/shard_map/ppermute | solution.py:31
  102.1 20.2 %all-to-all-start.2 = ((bf16[8,128,512]{2,1,0:T(8,128)(2,1)}), bf16[8,128,512]{2,1,0:T(8,128)(2,1)S(1)}, u32[]{:S(2)}, u32[]{:S(2)}) async-start(bf16[8,128,512]{2,1,0:T(8,128)(2,1)} %shard_map.130), calls=%async_computation.2 | async-start | bytes 2097152 | tf_op jit(solution)/shard_map/all_to_all | solution.py:35
  107.7 15.4 %collective-permute-start.22 = (bf16[1024,256]{1,0:T(8,128)(2,1)S(1)}, bf16[1024,256]{1,0:T(8,128)(2,1)S(1)}, u32[]{:S(2)}, u32[]{:S(2)}) collective-permute-start(bf16[1024,256]{1,0:T(8,128)(2,1)S(1)} %get-tuple-element.62), channel_id=1, source_target_pairs={{0,16},{1,17},{2,18},{3,19},{4,20},{5,21},{6,22},{7,23},{8,24},{9,... | collective-permute-start | bytes 1572872 | tf_op jit(solution)/shard_map/ppermute | solution.py:31
  108.7 14.4 %collective-permute-start.23 = (bf16[1024,256]{1,0:T(8,128)(2,1)S(1)}, bf16[1024,256]{1,0:T(8,128)(2,1)S(1)}, u32[]{:S(2)}, u32[]{:S(2)}) collective-permute-start(bf16[1024,256]{1,0:T(8,128)(2,1)S(1)} %get-tuple-element.63), channel_id=1, source_target_pairs={{0,48},{1,49},{2,50},{3,51},{4,52},{5,53},{6,54},{7,55},{8,56},{9,... | collective-permute-start | bytes 1572872 | tf_op jit(solution)/shard_map/ppermute | solution.py:31
  (14 other events, 18.7 us)

commit v2 on v1

--- a/solution.py
+++ b/solution.py
@@ -268,17 +268,17 @@
     pairs = [((rows_any, rows_oth)[i // 4].at[i % 4], rows_ref.at[i]) for i in range(8)]
     row_copies = fetch(pairs, row_sems)
     pairs = []
-    for i in range(16):
-        row = (cc * 8 + i) % 16 * 512
-        pairs.append((wq_any.at[pl.ds(pl.multiple_of(row, 512), 512)], wq_ref.at[pl.ds(i * 512, 512)]))
+    for i in range(4):
+        row = (cc * 2 + i) % 4 * 2048
+        pairs.append((wq_any.at[pl.ds(pl.multiple_of(row, 2048), 2048)], wq_ref.at[pl.ds(i * 2048, 2048)]))
     wq_copies = fetch(pairs, wq_sems)
     kv_copies = fetch([(half_any, half_ref), (other_any, other_ref)], kv_sems)
-    wo_copies = fetch([(wo_any.at[pl.ds(i * 16, 16)], wo_ref.at[pl.ds(i * 16, 16)]) for i in range(16)], wo_sems)
+    wo_copies = fetch([(wo_any.at[pl.ds(i * 64, 64)], wo_ref.at[pl.ds(i * 64, 64)]) for i in range(4)], wo_sems)
     queries = jnp.zeros((STEPS, 256), F32)
     for i in range(8):
         row_copies[i].wait()
-        wq_copies[2 * i].wait()
-        wq_copies[2 * i + 1].wait()
+        if i % 2 == 0:
+            wq_copies[i // 2].wait()
         queries += jnp.dot(rows_ref[i], wq_ref[i * 1024:(i + 1) * 1024, :], preferred_element_type=F32)
     queries = queries.astype(BF16)
     for copy in kv_copies:

time: 126 us -> 126 us (level)
  no operation moved by 1% of the time
where the time goes in v2:
time: 126 us
  starting transfers between devices  45.5 us (36%)
  Pallas kernels  41.4 us (33%)
  waiting for transfers between devices  30.7 us (24%)
  local copies, waits for them, and re-layouts  6.77 us (5%)
    pallas_call x17, Pallas kernels, call(): pl.pallas_call(body, out_shape=outs, cost_estimate=pl.CostEstimate(flops=...  41.4 us
    ppermute x24, starting transfers between devices, send(): return lax.ppermute(value, AXES, pairs)  33.3 us
    ppermute x24, waiting for transfers between devices, send(): return lax.ppermute(value, AXES, pairs)  27.4 us
    all_to_all x3, starting transfers between devices, swap_all(): lax.all_to_all(value, axis, split_axis=0, concat_axis=0, axis_index_group...  12.2 us
    unnamed x22, local copies, waits for them, and re-layouts  6.77 us
    all_to_all x3, waiting for transfers between devices, swap_all(): lax.all_to_all(value, axis, split_axis=0, concat_axis=0, axis_index_group...  3.25 us
  transfers between devices with their start and end apart: 27, of which 8 were waited for; matrix products, arithmetic and copies ran while one was open for 0% of the time, Pallas kernels for 31%

profile of v2, /device:TPU:1, one launch (start us, length us, event | category | flops | bytes accessed | tf_op | source)
XLA Modules:
  0.0 125.5 jit_solution(10813030331829590484)
XLA Ops:
  2.1 1.7 %collective-permute-start.5 = (bf16[96,8192]{1,0:T(8,128)(2,1)}, bf16[96,8192]{1,0:T(8,128)(2,1)}, u32[]{:S(2)}, u32[]{:S(2)}) collective-permute-start(bf16[96,8192]{1,0:T(8,128)(2,1)} %own.1), channel_id=1, source_target_pairs={{0,8},{1,9},{2,10},{3,11},{4,12},{5,13},{6,14},{7,15},{8,0},{9,1},... | collective-permute-start | bytes 4718600 | tf_op jit(solution)/shard_map/ppermute | solution.py:31
  7.7 5.1 %shard_map.121 = bf16[4,192,1024]{2,1,0:T(8,128)(2,1)} custom-call(bf16[64,4096]{1,0:T(8,128)(2,1)} %w_any.1, bf16[64,4096]{1,0:T(8,128)(2,1)} %g_any.1, f32[64,4096]{1,0:T(8,128)} %m_any.1, f32[64,4096]{1,0:T(8,128)} %s_any.1, bf16[96,8192]{1,0:T(8,128)(2,1)} %own.1, bf16[96,8192]{1,0:T(8,128)(2,1)} %copy-done.7, s32[1,128]{1,0:T(1,128)} %bound_ref.3), custom_call_target="tpu_custom_call" | custom-call | flops 4000000000 | tf_op jit(solution)/shard_map/pallas_call | solution.py:85
  12.8 3.6 %all-to-all-start = ((bf16[4,192,1024]{2,1,0:T(8,128)(2,1)}), bf16[4,192,1024]{2,1,0:T(8,128)(2,1)S(1)}, u32[]{:S(2)}, u32[]{:S(2)}) async-start(bf16[4,192,1024]{2,1,0:T(8,128)(2,1)} %shard_map.121), calls=%async_computation | async-start | bytes 3145728 | tf_op jit(solution)/shard_map/all_to_all | solution.py:35
  16.4 2.1 %collective-permute-done.1.top_any.k3 = bf16[32,8192]{1,0:T(8,128)(2,1)S(1)} collective-permute-done((bf16[32,8192]{1,0:T(8,128)(2,1)}, bf16[32,8192]{1,0:T(8,128)(2,1)S(1)}, u32[]{:S(2)}, u32[]{:S(2)}) %collective-permute-start.1) | collective-permute-done | bytes 524320 | tf_op jit(solution)/shard_map/ppermute | solution.py:31
  19.3 2.3 %shard_map.122 = bf16[64,8192]{1,0:T(8,128)(2,1)} custom-call(bf16[32,8192]{1,0:T(8,128)(2,1)} %copy-done.9, bf16[32,8192]{1,0:T(8,128)(2,1)} %bitcast.20), custom_call_target="tpu_custom_call" | custom-call | flops 8000000000 | tf_op jit(solution)/shard_map/pallas_call | solution.py:85
  21.8 2.5 %collective-permute-start.7 = (bf16[32,8192]{1,0:T(8,128)(2,1)S(1)}, bf16[32,8192]{1,0:T(8,128)(2,1)}, u32[]{:S(2)}, u32[]{:S(2)}) collective-permute-start(bf16[32,8192]{1,0:T(8,128)(2,1)S(1)} %bitcast.22), channel_id=1, source_target_pairs={{0,6},{1,7},{2,0},{3,1},{4,2},{5,3},{6,4},{7,5},{8,14},{9,15},{10,... | collective-permute-start | bytes 1572872 | tf_op jit(solution)/shard_map/ppermute | solution.py:31
  24.3 14.5 %collective-permute-done.5.zown = bf16[96,8192]{1,0:T(8,128)(2,1)} collective-permute-done((bf16[96,8192]{1,0:T(8,128)(2,1)}, bf16[96,8192]{1,0:T(8,128)(2,1)}, u32[]{:S(2)}, u32[]{:S(2)}) %collective-permute-start.5) | collective-permute-done | bytes 1572896 | tf_op jit(solution)/shard_map/ppermute | solution.py:31
  42.0 6.6 %collective-permute-done.3.got_any = bf16[512,256]{1,0:T(8,128)(2,1)S(1)} collective-permute-done((bf16[512,256]{1,0:T(8,128)(2,1)S(1)}, bf16[512,256]{1,0:T(8,128)(2,1)S(1)}, u32[]{:S(2)}, u32[]{:S(2)}) %collective-permute-start.3) | collective-permute-done | bytes 262176 | tf_op jit(solution)/shard_map/ppermute | solution.py:31
  49.8 2.5 %collective-permute-start.9 = (bf16[32,8192]{1,0:T(8,128)(2,1)}, bf16[32,8192]{1,0:T(8,128)(2,1)S(1)}, u32[]{:S(2)}, u32[]{:S(2)}) collective-permute-start(bf16[32,8192]{1,0:T(8,128)(2,1)} %collective-permute-done.7.v1), channel_id=1, source_target_pairs={{0,6},{1,7},{2,0},{3,1},{4,2},{5,3},{6,4},{7,5},{8,14},{9,15},{10,... | collective-permute-start | bytes 1572872 | tf_op jit(solution)/shard_map/ppermute | solution.py:31
  56.7 2.2 %collective-permute-start.13 = (bf16[512,256]{1,0:T(8,128)(2,1)S(1)}, bf16[512,256]{1,0:T(8,128)(2,1)S(1)}, u32[]{:S(2)}, u32[]{:S(2)}) collective-permute-start(bf16[512,256]{1,0:T(8,128)(2,1)S(1)} %get-tuple-element.50), channel_id=1, source_target_pairs={{0,72},{1,73},{2,74},{3,75},{4,76},{5,77},{6,78},{7,79},{8,64},{9,... | collective-permute-start | bytes 786440 | tf_op jit(solution)/shard_map/ppermute | solution.py:31
  58.9 4.2 %all-to-all-start.1 = ((bf16[4,128,1024]{2,1,0:T(8,128)(2,1)}), bf16[4,128,1024]{2,1,0:T(8,128)(2,1)}, u32[]{:S(2)}, u32[]{:S(2)}) async-start(bf16[4,128,1024]{2,1,0:T(8,128)(2,1)} %shard_map.124), calls=%async_computation.1 | async-start | bytes 2097152 | tf_op jit(solution)/shard_map/all_to_all | solution.py:35
  65.1 6.0 %shard_map.125 = (bf16[128,384]{1,0:T(8,128)(2,1)}, bf16[128,384]{1,0:T(8,128)(2,1)}, bf16[128,384]{1,0:T(8,128)(2,1)}, bf16[128,384]{1,0:T(8,128)(2,1)}) custom-call(bf16[96,8192]{1,0:T(8,128)(2,1)} %own.1, bf16[96,8192]{1,0:T(8,128)(2,1)} %copy-done.7, bf16[96,8192]{1,0:T(8,128)(2,1)} %collective-permute-done.5.zown, ...), custom_call_target="tpu_custom_call" | custom-call | flops 99999997952 | tf_op jit(solution)/shard_map/pallas_call | solution.py:85
  71.2 2.6 %collective-permute-start.14 = (bf16[128,384]{1,0:T(8,128)(2,1)}, bf16[128,384]{1,0:T(8,128)(2,1)S(1)}, u32[]{:S(2)}, u32[]{:S(2)}) collective-permute-start(bf16[128,384]{1,0:T(8,128)(2,1)} %get-tuple-element.53), channel_id=1, source_target_pairs={{0,6},{1,7},{2,0},{3,1},{4,2},{5,3},{6,4},{7,5},{8,14},{9,15},{10,... | collective-permute-start | bytes 294920 | tf_op jit(solution)/shard_map/ppermute | solution.py:31
  79.0 2.5 %collective-permute-start.4 = (bf16[4,128,1024]{2,1,0:T(8,128)(2,1)}, bf16[4,128,1024]{2,1,0:T(8,128)(2,1)S(1)}, u32[]{:S(2)}, u32[]{:S(2)}) collective-permute-start(bf16[4,128,1024]{2,1,0:T(8,128)(2,1)} %all-to-all-done.1.rows_any), channel_id=1, source_target_pairs={{0,1},{1,0},{2,3},{3,2},{4,5},{5,4},{6,7},{7,6},{8,9},{9,8},{10,11... | collective-permute-start | bytes 3145736 | tf_op jit(solution)/shard_map/ppermute | solution.py:31
  87.0 8.8 %shard_map.129 = (bf16[4,128,512]{2,1,0:T(8,128)(2,1)}, bf16[4,128,512]{2,1,0:T(8,128)(2,1)}, bf16[8,128,512]{2,1,0:T(8,128)(2,1)}) custom-call(bf16[4,128,1024]{2,1,0:T(8,128)(2,1)} %all-to-all-done.1.rows_any, bf16[4,128,1024]{2,1,0:T(8,128)(2,1)} %copy-done, bf16[8192,256]{1,0:T(8,128)(2,1)} %wq_any.1, bf16[128,1536]{1,0:T(8,128)(2,1)} %copy-done.1, ...), custom_call_target="tpu_custom_call" | custom-call | tf_op jit(solution)/shard_map/pallas_call | solution.py:85
  96.3 1.6 %collective-permute-done.18.got_a = bf16[4,128,512]{2,1,0:T(8,128)(2,1)S(1)} collective-permute-done((bf16[4,128,512]{2,1,0:T(8,128)(2,1)}, bf16[4,128,512]{2,1,0:T(8,128)(2,1)S(1)}, u32[]{:S(2)}, u32[]{:S(2)}) %collective-permute-start.18) | collective-permute-done | bytes 524320 | tf_op jit(solution)/shard_map/ppermute | solution.py:31
  99.5 2.5 %shard_map.130 = bf16[8,128,512]{2,1,0:T(8,128)(2,1)} custom-call(bf16[8,128,512]{2,1,0:T(8,128)(2,1)} %get-tuple-element.56.mine_any, bf16[4,128,512]{2,1,0:T(8,128)(2,1)} %copy-done.4, bf16[4,128,512]{2,1,0:T(8,128)(2,1)} %copy-done.5), custom_call_target="tpu_custom_call" | custom-call | tf_op jit(solution)/shard_map/pallas_call | solution.py:85
  102.0 4.4 %all-to-all-start.2 = ((bf16[8,128,512]{2,1,0:T(8,128)(2,1)}), bf16[8,128,512]{2,1,0:T(8,128)(2,1)S(1)}, u32[]{:S(2)}, u32[]{:S(2)}) async-start(bf16[8,128,512]{2,1,0:T(8,128)(2,1)} %shard_map.130), calls=%async_computation.2 | async-start | bytes 2097152 | tf_op jit(solution)/shard_map/all_to_all | solution.py:35
  108.6 1.7 %collective-permute-start.23 = (bf16[1024,256]{1,0:T(8,128)(2,1)S(1)}, bf16[1024,256]{1,0:T(8,128)(2,1)S(1)}, u32[]{:S(2)}, u32[]{:S(2)}) collective-permute-start(bf16[1024,256]{1,0:T(8,128)(2,1)S(1)} %get-tuple-element.63), channel_id=1, source_target_pairs={{0,48},{1,49},{2,50},{3,51},{4,52},{5,53},{6,54},{7,55},{8,56},{9,... | collective-permute-start | bytes 1572872 | tf_op jit(solution)/shard_map/ppermute | solution.py:31
  110.5 2.8 %shard_map.134 = (bf16[8192,256]{1,0:T(8,128)(2,1)}, f32[2,64]{1,0:T(2,128)S(1)}) custom-call(s32[4]{0:T(128)S(1)} %get-tuple-element.75.at_ref, bf16[2,2,2,4,64,256]{5,4,3,2,1,0:T(8,128)(2,1)} %bitcast.13.refs_0_.refs_1_, bf16[2,2,2,4,64,256]{5,4,3,2,1,0:T(8,128)(2,1)} %bitcast.13.refs_0_.refs_1_), custom_call_target="tpu_custom_call" | custom-call | tf_op jit(solution)/shard_map/pallas_call | solution.py:85
  113.3 2.8 %shard_map.135 = (bf16[8192,256]{1,0:T(8,128)(2,1)}, f32[2,64]{1,0:T(2,128)S(1)}) custom-call(s32[4]{0:T(128)S(1)} %get-tuple-element.77.at_ref, bf16[2,2,2,4,64,256]{5,4,3,2,1,0:T(8,128)(2,1)} %bitcast.11.refs_0_.refs_1_, bf16[2,2,2,4,64,256]{5,4,3,2,1,0:T(8,128)(2,1)} %bitcast.11.refs_0_.refs_1_, ...), custom_call_target="tpu_custom_call", output_to_operand_aliasing={{0}: (3, {})} | custom-call | tf_op jit(solution)/shard_map/pallas_call | solution.py:85
  116.2 2.8 %shard_map.136 = (bf16[8192,256]{1,0:T(8,128)(2,1)}, f32[2,64]{1,0:T(2,128)S(1)}) custom-call(s32[4]{0:T(128)S(1)} %get-tuple-element.78.at_ref, bf16[2,2,2,4,64,256]{5,4,3,2,1,0:T(8,128)(2,1)} %bitcast.9.refs_0_.refs_1_, bf16[2,2,2,4,64,256]{5,4,3,2,1,0:T(8,128)(2,1)} %bitcast.9.refs_0_.refs_1_, ...), custom_call_target="tpu_custom_call", output_to_operand_aliasing={{0}: (3, {})} | custom-call | tf_op jit(solution)/shard_map/pallas_call | solution.py:85
  119.0 3.2 %all-to-all-done.2.got_ref = bf16[8,128,512]{2,1,0:T(8,128)(2,1)S(1)} async-done(((bf16[8,128,512]{2,1,0:T(8,128)(2,1)}), bf16[8,128,512]{2,1,0:T(8,128)(2,1)S(1)}, u32[]{:S(2)}, u32[]{:S(2)}) %all-to-all-start.2) | async-done | bytes 1048608 | tf_op jit(solution)/shard_map/all_to_all | solution.py:35
  123.0 2.4 %shard_map.137 = (bf16[8192,256]{1,0:T(8,128)(2,1)}, f32[2,64]{1,0:T(2,128)}) custom-call(s32[4]{0:T(128)S(1)} %get-tuple-element.79.at_ref, bf16[1,2,2,4,64,256]{5,4,3,2,1,0:T(8,128)(2,1)S(1)} %bitcast.15, bf16[1,2,2,4,64,256]{5,4,3,2,1,0:T(8,128)(2,1)S(1)} %bitcast.16, ...), custom_call_target="tpu_custom_call", output_to_operand_aliasing={{0}: (3, {})} | custom-call | tf_op jit(solution)/shard_map/pallas_call | solution.py:85
  (71 shorter events, 33.0 us)
Async XLA Ops:
  0.6 5.9 %collective-permute-start = (bf16[96,8192]{1,0:T(8,128)(2,1)}, bf16[96,8192]{1,0:T(8,128)(2,1)S(1)}, u32[]{:S(2)}, u32[]{:S(2)}) collective-permute-start(bf16[96,8192]{1,0:T(8,128)(2,1)} %own.1), channel_id=1, source_target_pairs={{0,1},{1,0},{2,3},{3,2},{4,5},{5,4},{6,7},{7,6},{8,9},{9,8},{10,11... | collective-permute-start | bytes 4718600 | tf_op jit(solution)/shard_map/ppermute | solution.py:31
  2.1 36.7 %collective-permute-start.5 = (bf16[96,8192]{1,0:T(8,128)(2,1)}, bf16[96,8192]{1,0:T(8,128)(2,1)}, u32[]{:S(2)}, u32[]{:S(2)}) collective-permute-start(bf16[96,8192]{1,0:T(8,128)(2,1)} %own.1), channel_id=1, source_target_pairs={{0,8},{1,9},{2,10},{3,11},{4,12},{5,13},{6,14},{7,15},{8,0},{9,1},... | collective-permute-start | bytes 4718600 | tf_op jit(solution)/shard_map/ppermute | solution.py:31
  3.9 14.6 %collective-permute-start.1 = (bf16[32,8192]{1,0:T(8,128)(2,1)}, bf16[32,8192]{1,0:T(8,128)(2,1)S(1)}, u32[]{:S(2)}, u32[]{:S(2)}) collective-permute-start(bf16[32,8192]{1,0:T(8,128)(2,1)} %bitcast.17), channel_id=1, source_target_pairs={{0,2},{1,3},{2,4},{3,5},{4,6},{5,7},{6,0},{7,1},{8,10},{9,11},{10,... | collective-permute-start | bytes 1572872 | tf_op jit(solution)/shard_map/ppermute | solution.py:31
  5.1 13.4 %collective-permute-start.2 = (bf16[32,8192]{1,0:T(8,128)(2,1)}, bf16[32,8192]{1,0:T(8,128)(2,1)}, u32[]{:S(2)}, u32[]{:S(2)}) collective-permute-start(bf16[32,8192]{1,0:T(8,128)(2,1)} %bitcast.18), channel_id=1, source_target_pairs={{0,6},{1,7},{2,0},{3,1},{4,2},{5,3},{6,4},{7,5},{8,14},{9,15},{10,... | collective-permute-start | bytes 1572872 | tf_op jit(solution)/shard_map/ppermute | solution.py:31
  12.8 26.7 %all-to-all-start = ((bf16[4,192,1024]{2,1,0:T(8,128)(2,1)}), bf16[4,192,1024]{2,1,0:T(8,128)(2,1)S(1)}, u32[]{:S(2)}, u32[]{:S(2)}) async-start(bf16[4,192,1024]{2,1,0:T(8,128)(2,1)} %shard_map.121), calls=%async_computation | async-start | bytes 3145728 | tf_op jit(solution)/shard_map/all_to_all | solution.py:35
  21.5 42.8 %collective-permute-start.8 = (bf16[64,8192]{1,0:T(8,128)(2,1)}, bf16[64,8192]{1,0:T(8,128)(2,1)}, u32[]{:S(2)}, u32[]{:S(2)}) collective-permute-start(bf16[64,8192]{1,0:T(8,128)(2,1)} %shard_map.122), channel_id=1, source_target_pairs={{0,2},{1,3},{2,4},{3,5},{4,6},{5,7},{6,0},{7,1},{8,10},{9,11},{10,... | collective-permute-start | bytes 3145736 | tf_op jit(solution)/shard_map/ppermute | solution.py:31
  21.8 28.0 %collective-permute-start.7 = (bf16[32,8192]{1,0:T(8,128)(2,1)S(1)}, bf16[32,8192]{1,0:T(8,128)(2,1)}, u32[]{:S(2)}, u32[]{:S(2)}) collective-permute-start(bf16[32,8192]{1,0:T(8,128)(2,1)S(1)} %bitcast.22), channel_id=1, source_target_pairs={{0,6},{1,7},{2,0},{3,1},{4,2},{5,3},{6,4},{7,5},{8,14},{9,15},{10,... | collective-permute-start | bytes 1572872 | tf_op jit(solution)/shard_map/ppermute | solution.py:31
  38.8 24.4 %collective-permute-start.6 = (bf16[96,8192]{1,0:T(8,128)(2,1)}, bf16[96,8192]{1,0:T(8,128)(2,1)}, u32[]{:S(2)}, u32[]{:S(2)}) collective-permute-start(bf16[96,8192]{1,0:T(8,128)(2,1)} %collective-permute-done.5.zown), channel_id=1, source_target_pairs={{0,1},{1,0},{2,3},{3,2},{4,5},{5,4},{6,7},{7,6},{8,9},{9,8},{10,11... | collective-permute-start | bytes 4718600 | tf_op jit(solution)/shard_map/ppermute | solution.py:31
  40.4 8.2 %collective-permute-start.3 = (bf16[512,256]{1,0:T(8,128)(2,1)S(1)}, bf16[512,256]{1,0:T(8,128)(2,1)S(1)}, u32[]{:S(2)}, u32[]{:S(2)}) collective-permute-start(bf16[512,256]{1,0:T(8,128)(2,1)S(1)} %get-tuple-element.41.mine_any), channel_id=1, source_target_pairs={{0,8},{1,9},{2,10},{3,11},{4,12},{5,13},{6,14},{7,15},{8,0},{9,1},... | collective-permute-start | bytes 786440 | tf_op jit(solution)/shard_map/ppermute | solution.py:31
  49.8 14.5 %collective-permute-start.9 = (bf16[32,8192]{1,0:T(8,128)(2,1)}, bf16[32,8192]{1,0:T(8,128)(2,1)S(1)}, u32[]{:S(2)}, u32[]{:S(2)}) collective-permute-start(bf16[32,8192]{1,0:T(8,128)(2,1)} %collective-permute-done.7.v1), channel_id=1, source_target_pairs={{0,6},{1,7},{2,0},{3,1},{4,2},{5,3},{6,4},{7,5},{8,14},{9,15},{10,... | collective-permute-start | bytes 1572872 | tf_op jit(solution)/shard_map/ppermute | solution.py:31
  55.1 19.2 %collective-permute-start.11 = (bf16[512,256]{1,0:T(8,128)(2,1)S(1)}, bf16[512,256]{1,0:T(8,128)(2,1)S(1)}, u32[]{:S(2)}, u32[]{:S(2)}) collective-permute-start(bf16[512,256]{1,0:T(8,128)(2,1)S(1)} %get-tuple-element.50), channel_id=1, source_target_pairs={{0,8},{1,9},{2,10},{3,11},{4,12},{5,13},{6,14},{7,15},{8,0},{9,1},... | collective-permute-start | bytes 786440 | tf_op jit(solution)/shard_map/ppermute | solution.py:31
  56.7 18.3 %collective-permute-start.13 = (bf16[512,256]{1,0:T(8,128)(2,1)S(1)}, bf16[512,256]{1,0:T(8,128)(2,1)S(1)}, u32[]{:S(2)}, u32[]{:S(2)}) collective-permute-start(bf16[512,256]{1,0:T(8,128)(2,1)S(1)} %get-tuple-element.50), channel_id=1, source_target_pairs={{0,72},{1,73},{2,74},{3,75},{4,76},{5,77},{6,78},{7,79},{8,64},{9,... | collective-permute-start | bytes 786440 | tf_op jit(solution)/shard_map/ppermute | solution.py:31
  58.9 20.0 %all-to-all-start.1 = ((bf16[4,128,1024]{2,1,0:T(8,128)(2,1)}), bf16[4,128,1024]{2,1,0:T(8,128)(2,1)}, u32[]{:S(2)}, u32[]{:S(2)}) async-start(bf16[4,128,1024]{2,1,0:T(8,128)(2,1)} %shard_map.124), calls=%async_computation.1 | async-start | bytes 2097152 | tf_op jit(solution)/shard_map/all_to_all | solution.py:35
  63.2 11.8 %collective-permute-start.12 = (bf16[512,256]{1,0:T(8,128)(2,1)S(1)}, bf16[512,256]{1,0:T(8,128)(2,1)S(1)}, u32[]{:S(2)}, u32[]{:S(2)}) collective-permute-start(bf16[512,256]{1,0:T(8,128)(2,1)S(1)} %get-tuple-element.51.refs_0_), channel_id=1, source_target_pairs={{0,64},{1,65},{2,66},{3,67},{4,68},{5,69},{6,70},{7,71},{8,72},{9,... | collective-permute-start | bytes 786440 | tf_op jit(solution)/shard_map/ppermute | solution.py:31
  71.2 7.8 %collective-permute-start.14 = (bf16[128,384]{1,0:T(8,128)(2,1)}, bf16[128,384]{1,0:T(8,128)(2,1)S(1)}, u32[]{:S(2)}, u32[]{:S(2)}) collective-permute-start(bf16[128,384]{1,0:T(8,128)(2,1)} %get-tuple-element.53), channel_id=1, source_target_pairs={{0,6},{1,7},{2,0},{3,1},{4,2},{5,3},{6,4},{7,5},{8,14},{9,15},{10,... | collective-permute-start | bytes 294920 | tf_op jit(solution)/shard_map/ppermute | solution.py:31
  73.8 7.6 %collective-permute-start.15 = (bf16[128,384]{1,0:T(8,128)(2,1)}, bf16[128,384]{1,0:T(8,128)(2,1)S(1)}, u32[]{:S(2)}, u32[]{:S(2)}) collective-permute-start(bf16[128,384]{1,0:T(8,128)(2,1)} %get-tuple-element.54), channel_id=1, source_target_pairs={{0,4},{1,5},{2,6},{3,7},{4,0},{5,1},{6,2},{7,3},{8,12},{9,13},{10,... | collective-permute-start | bytes 294920 | tf_op jit(solution)/shard_map/ppermute | solution.py:31
  74.4 7.7 %collective-permute-start.16 = (bf16[128,384]{1,0:T(8,128)(2,1)}, bf16[128,384]{1,0:T(8,128)(2,1)S(1)}, u32[]{:S(2)}, u32[]{:S(2)}) collective-permute-start(bf16[128,384]{1,0:T(8,128)(2,1)} %get-tuple-element.55), channel_id=1, source_target_pairs={{0,2},{1,3},{2,4},{3,5},{4,6},{5,7},{6,0},{7,1},{8,10},{9,11},{10,... | collective-permute-start | bytes 294920 | tf_op jit(solution)/shard_map/ppermute | solution.py:31
  76.1 30.3 %collective-permute-start.20 = (bf16[2048,256]{1,0:T(8,128)(2,1)}, bf16[2048,256]{1,0:T(8,128)(2,1)}, u32[]{:S(2)}, u32[]{:S(2)}) collective-permute-start(bf16[2048,256]{1,0:T(8,128)(2,1)} %shard_map.132), channel_id=1, source_target_pairs={{0,16},{1,17},{2,18},{3,19},{4,20},{5,21},{6,22},{7,23},{8,24},{9,... | collective-permute-start | bytes 3145736 | tf_op jit(solution)/shard_map/ppermute | solution.py:31
  77.4 28.9 %collective-permute-start.21 = (bf16[2048,256]{1,0:T(8,128)(2,1)}, bf16[2048,256]{1,0:T(8,128)(2,1)}, u32[]{:S(2)}, u32[]{:S(2)}) collective-permute-start(bf16[2048,256]{1,0:T(8,128)(2,1)} %shard_map.132), channel_id=1, source_target_pairs={{0,48},{1,49},{2,50},{3,51},{4,52},{5,53},{6,54},{7,55},{8,56},{9,... | collective-permute-start | bytes 3145736 | tf_op jit(solution)/shard_map/ppermute | solution.py:31
  79.0 5.7 %collective-permute-start.4 = (bf16[4,128,1024]{2,1,0:T(8,128)(2,1)}, bf16[4,128,1024]{2,1,0:T(8,128)(2,1)S(1)}, u32[]{:S(2)}, u32[]{:S(2)}) collective-permute-start(bf16[4,128,1024]{2,1,0:T(8,128)(2,1)} %all-to-all-done.1.rows_any), channel_id=1, source_target_pairs={{0,1},{1,0},{2,3},{3,2},{4,5},{5,4},{6,7},{7,6},{8,9},{9,8},{10,11... | collective-permute-start | bytes 3145736 | tf_op jit(solution)/shard_map/ppermute | solution.py:31
  83.1 3.1 %collective-permute-start.17 = (bf16[128,1536]{1,0:T(8,128)(2,1)S(1)}, bf16[128,1536]{1,0:T(8,128)(2,1)S(1)}, u32[]{:S(2)}, u32[]{:S(2)}) collective-permute-start(bf16[128,1536]{1,0:T(8,128)(2,1)S(1)} %shard_map.127.half_any), channel_id=1, source_target_pairs={{0,1},{1,0},{2,3},{3,2},{4,5},{5,4},{6,7},{7,6},{8,9},{9,8},{10,11... | collective-permute-start | bytes 1179656 | tf_op jit(solution)/shard_map/ppermute | solution.py:31
  102.0 20.2 %all-to-all-start.2 = ((bf16[8,128,512]{2,1,0:T(8,128)(2,1)}), bf16[8,128,512]{2,1,0:T(8,128)(2,1)S(1)}, u32[]{:S(2)}, u32[]{:S(2)}) async-start(bf16[8,128,512]{2,1,0:T(8,128)(2,1)} %shard_map.130), calls=%async_computation.2 | async-start | bytes 2097152 | tf_op jit(solution)/shard_map/all_to_all | solution.py:35
  107.6 15.4 %collective-permute-start.22 = (bf16[1024,256]{1,0:T(8,128)(2,1)S(1)}, bf16[1024,256]{1,0:T(8,128)(2,1)S(1)}, u32[]{:S(2)}, u32[]{:S(2)}) collective-permute-start(bf16[1024,256]{1,0:T(8,128)(2,1)S(1)} %get-tuple-element.62), channel_id=1, source_target_pairs={{0,16},{1,17},{2,18},{3,19},{4,20},{5,21},{6,22},{7,23},{8,24},{9,... | collective-permute-start | bytes 1572872 | tf_op jit(solution)/shard_map/ppermute | solution.py:31
  108.6 14.4 %collective-permute-start.23 = (bf16[1024,256]{1,0:T(8,128)(2,1)S(1)}, bf16[1024,256]{1,0:T(8,128)(2,1)S(1)}, u32[]{:S(2)}, u32[]{:S(2)}) collective-permute-start(bf16[1024,256]{1,0:T(8,128)(2,1)S(1)} %get-tuple-element.63), channel_id=1, source_target_pairs={{0,48},{1,49},{2,50},{3,51},{4,52},{5,53},{6,54},{7,55},{8,56},{9,... | collective-permute-start | bytes 1572872 | tf_op jit(solution)/shard_map/ppermute | solution.py:31
  (14 other events, 18.7 us)
